TPU v7x, 32 devices: a whole 2x2x4 slice. The times are simulated.
32 devices in a mesh: ctx: 8 (over z, y), tp: 4 (over x, core).
Axes of the slice: x: 2, y: 2, z: 4, core: 2. Of those that a mesh axis runs over, the one named last changes fastest.
Arguments:
- queries: bfloat16 [1024, 12288], P('ctx', 'tp'), may hold values from -8 to 8
- keys: bfloat16 [1024, 1024], P('ctx'), may hold values from -16 to 16
- values: bfloat16 [1024, 1024], P('ctx'), may hold values from -6 to 6
- doc_ids: int32 [1024], replicated, may hold values from 0 to 3, never falling along the last dimension, each value on 1 to 640 neighbouring positions
- replica_of: int32 [4], replicated, may hold values from 0 to 7, as said below
- step_query: bfloat16 [4, 12288], P(None, 'tp'), may hold values from -8 to 8
- step_key: bfloat16 [4, 1024], replicated, may hold values from -16 to 16
- step_value: bfloat16 [4, 1024], replicated, may hold values from -6 to 6
- out_weight: bfloat16 [12288, 12288], P('tp', 'ctx'), may hold values from -0.0546875 to 0.0546875
Outputs:
- context: bfloat16 [1024, 12288], P('ctx', 'tp')
- next_hidden: bfloat16 [8, 12288], P(None, 'ctx')
- replica_keys: bfloat16 [8, 1024, 640], P('ctx', 'tp')
- replica_values: bfloat16 [8, 1024, 640], P('ctx', 'tp')
Inputs may be any that keep to these rules, and one draw needn't show every extreme that they name: `doc_ids`: documents occupy whole runs of positions in rising order; each has 1 to 640 positions, and one has exactly 640. `replica_of`: the documents name distinct replicas.
All inputs are finite; a program needn't handle non-finite values.
Results may differ from a plain program's by a relative error of at most 0.02.
Values may be sent and summed in bfloat16 or wider, within the bound.
A program may use at most 64 MiB of HBM per device.

v0:
```python
import math

import jax
import jax.numpy as jnp
from jax import lax
from jax.sharding import PartitionSpec as P

H = 96
KVH = 8
HD = 128


def local(queries, keys, values, doc_ids, replica_of, step_query, step_key, step_value, out_weight):
    row_count = queries.shape[0]
    heads_dev = queries.shape[1] // HD
    group_size = H // KVH
    kv_dev = max(1, heads_dev // group_size)
    per_kv = heads_dev // kv_dev
    score_scale = 1.0 / math.sqrt(HD)
    cache_most = 5 * (row_count * lax.axis_size("ctx")) // 8
    column_width = keys.shape[1] // lax.axis_size("tp")
    ctx_index = lax.axis_index("ctx")
    tp_index = lax.axis_index("tp")
    first_kv = tp_index * heads_dev // group_size
    column_offset = tp_index * column_width - first_kv * HD
    key_own = lax.dynamic_slice_in_dim(keys, first_kv * HD, kv_dev * HD, 1)
    value_own = lax.dynamic_slice_in_dim(values, first_kv * HD, kv_dev * HD, 1)
    query_pos = ctx_index * row_count + jnp.arange(row_count, dtype=jnp.int32)
    query_doc = lax.dynamic_slice_in_dim(doc_ids, ctx_index * row_count, row_count, 0)
    grouped = queries.reshape(row_count, kv_dev, per_kv, HD).transpose(1, 2, 0, 3)
    grouped = grouped.reshape(kv_dev, per_kv * row_count, HD)
    row_pos = jnp.tile(query_pos, per_kv)
    row_doc = jnp.tile(query_doc, per_kv)
    match_rows = (replica_of == ctx_index).astype(jnp.int32)
    has_request = jnp.sum(match_rows) > 0
    my_doc = jnp.sum(match_rows * jnp.arange(replica_of.shape[0], dtype=jnp.int32))
    doc_start = jnp.sum((doc_ids < my_doc).astype(jnp.int32))
    doc_length = jnp.sum((doc_ids == my_doc).astype(jnp.int32))
    attend_init = (
        jnp.full((kv_dev, per_kv * row_count), -1e30, jnp.float32),
        jnp.zeros((kv_dev, per_kv * row_count), jnp.float32),
        jnp.zeros((kv_dev, per_kv * row_count, HD), jnp.float32),
    )
    cache_init = (
        jnp.zeros((cache_most, kv_dev * HD), jnp.bfloat16),
        jnp.zeros((cache_most, kv_dev * HD), jnp.bfloat16),
    )
    key_piece = lax.all_gather(key_own, "ctx", axis=0, tiled=True)
    value_piece = lax.all_gather(value_own, "ctx", axis=0, tiled=True)
    piece_rows = key_piece.shape[0]
    key_pos = jnp.arange(piece_rows, dtype=jnp.int32)
    key_doc = doc_ids
    allowed = (key_doc[None, :] == row_doc[:, None]) & (key_pos[None, :] <= row_pos[:, None])

    def update(old_state):
        row_top, row_total, accumulated = old_state
        key_heads = key_piece.reshape(piece_rows, kv_dev, HD)
        value_heads = value_piece.reshape(piece_rows, kv_dev, HD)
        scores = (
            jnp.einsum("kqd,pkd->kqp", grouped, key_heads, preferred_element_type=jnp.float32)
            * score_scale
        )
        masked = jnp.where(allowed[None], scores, -1e30)
        new_top = jnp.maximum(row_top, jnp.max(masked, axis=-1))
        weights = jnp.where(allowed[None], jnp.exp(scores - new_top[..., None]), 0.0)
        row_total = jnp.sum(weights, axis=-1)
        added = jnp.einsum(
            "kqp,pkd->kqd",
            weights.astype(jnp.bfloat16),
            value_heads,
            preferred_element_type=jnp.float32,
        )
        accumulated = added
        return (new_top, row_total, accumulated)

    attend_state = lax.cond(jnp.any(allowed), update, lambda old_state: old_state, attend_init)
    place_key_piece = lax.all_gather(key_own, "ctx", axis=0, tiled=True)
    place_value_piece = lax.all_gather(value_own, "ctx", axis=0, tiled=True)
    place_piece_rows = place_key_piece.shape[0]
    key_pos = jnp.arange(place_piece_rows, dtype=jnp.int32)
    key_doc = doc_ids
    keep_rows = (key_doc == my_doc) & has_request
    offset = jnp.where(keep_rows, key_pos - doc_start, cache_most)
    cache_keys = cache_init[0].at[offset].set(place_key_piece, mode="drop")
    cache_values = cache_init[1].at[offset].set(place_value_piece, mode="drop")
    cache_state = (cache_keys, cache_values)
    row_top, row_total, accumulated = attend_state
    context = (accumulated / row_total[..., None]).reshape(kv_dev, per_kv, row_count, HD)
    context = context.transpose(2, 0, 1, 3).reshape(row_count, heads_dev * HD).astype(jnp.bfloat16)
    delivered_keys = lax.dynamic_slice_in_dim(cache_state[0], column_offset, column_width, 1)
    delivered_values = lax.dynamic_slice_in_dim(cache_state[1], column_offset, column_width, 1)
    replica_keys = jnp.transpose(delivered_keys, (1, 0))[None]
    replica_values = jnp.transpose(delivered_values, (1, 0))[None]
    cache_keys = cache_state[0].reshape(cache_most, kv_dev, HD)
    cache_values = cache_state[1].reshape(cache_most, kv_dev, HD)
    query_row = lax.dynamic_slice_in_dim(step_query, my_doc, 1, 0).reshape(kv_dev, per_kv, HD)
    own_key = lax.dynamic_slice(step_key, (my_doc, first_kv * HD), (1, kv_dev * HD)).reshape(
        kv_dev, HD
    )
    own_value = lax.dynamic_slice(step_value, (my_doc, first_kv * HD), (1, kv_dev * HD)).reshape(
        kv_dev, HD
    )
    cached = (
        jnp.einsum("kgd,mkd->kgm", query_row, cache_keys, preferred_element_type=jnp.float32)
        * score_scale
    )
    own_score = (
        jnp.einsum("kgd,kd->kg", query_row, own_key, preferred_element_type=jnp.float32)
        * score_scale
    )
    valid_slots = jnp.arange(cache_most, dtype=jnp.int32) < doc_length
    step_top = jnp.maximum(
        jnp.max(jnp.where(valid_slots[None, None], cached, -1e30), axis=-1), own_score
    )
    weights = jnp.where(valid_slots[None, None], jnp.exp(cached - step_top[..., None]), 0.0)
    own_prob = jnp.exp(own_score - step_top)
    step_total = jnp.sum(weights, axis=-1) + own_prob
    own_rounded = lax.optimization_barrier(own_prob.astype(jnp.bfloat16)).astype(jnp.float32)
    mixed_sum = jnp.einsum(
        "kgm,mkd->kgd",
        weights.astype(jnp.bfloat16),
        cache_values,
        preferred_element_type=jnp.float32,
    )
    mixed_sum = mixed_sum + own_rounded[..., None] * own_value.astype(jnp.float32)[:, None, :]
    decode_row = (mixed_sum / step_total[..., None]).reshape(1, heads_dev * HD)
    decode_row = jnp.where(has_request, decode_row, 0.0).astype(jnp.bfloat16)
    gathered = lax.all_gather(decode_row, "ctx", axis=0, tiled=True)
    partial_value = jnp.dot(gathered, out_weight, preferred_element_type=jnp.float32)
    next_hidden = lax.psum(partial_value.astype(jnp.bfloat16), "tp")
    return (context, next_hidden, replica_keys, replica_values)


def solution(mesh):
    placed = (
        P("ctx", "tp"),
        P("ctx", None),
        P("ctx", None),
        P(),
        P(),
        P(None, "tp"),
        P(),
        P(),
        P("tp", "ctx"),
    )
    return jax.shard_map(
        local,
        mesh=mesh,
        in_specs=placed,
        out_specs=(P("ctx", "tp"), P(None, "ctx"), P("ctx", "tp", None), P("ctx", "tp", None)),
        check_vma=False,
    )
```

profile of v0, /device:TPU:0, one launch (start us, length us, event | category | flops | bytes accessed | tf_op | source)
XLA Modules:
  0.0 166.8 jit_solution(16812356034072617578)
XLA Ops:
  0.7 0.8 dynamic_slice.20
  1.5 3.2 %fusion.12 = (pred[1536,1024]{0,1:T(8,128)(4,1)S(1)}, pred[]{:T(512)}) fusion(s32[1536]{0:T(1024)S(1)} %get-tuple-element.62, s32[1536]{0:T(1024)S(1)} %get-tuple-element.63, s32[1024]{0:T(1024)} %param.14), kind=kLoop, calls=%fused_computation.17 | loop fusion | flops 6291455 | bytes 1589249 | tf_op jit(solution)/shard_map/and | solution.py:53
  5.3 2.3 %copy.47 = bf16[128,3072]{0,1:T(8,128)(2,1)} copy(bf16[128,3072]{1,0:T(8,128)(2,1)} %param.11) | data formatting | bytes 1572864 | tf_op args[0]
  7.6 35.2 %all_gather.11 = bf16[1024,256]{1,0:T(8,128)(2,1)} all-gather(bf16[128,256]{1,0:T(8,128)(2,1)S(1)} %constant_dynamic-slice_fusion.1), channel_id=1, replica_groups=mesh['ctx'=8,'tp'=4] {'ctx'}, dimensions={0}, use_global_device_ids=true | all-gather | bytes 589824 | tf_op jit(solution)/shard_map/all_gather | solution.py:48
  42.9 0.8 constant_dynamic-slice_fusion
  43.7 33.2 %all_gather.12 = bf16[1024,256]{1,0:T(8,128)(2,1)} all-gather(bf16[128,256]{1,0:T(8,128)(2,1)S(1)} %constant_dynamic-slice_fusion), channel_id=1, replica_groups=mesh['ctx'=8,'tp'=4] {'ctx'}, dimensions={0}, use_global_device_ids=true | all-gather | bytes 589824 | tf_op jit(solution)/shard_map/all_gather | solution.py:49
  76.9 20.2 %conditional.1 = (f32[2,1536]{1,0:T(2,128)S(1)}, f32[2,1536,128]{2,1,0:T(8,128)S(1)}) conditional(s32[]{:T(128)} %convert_element_type.63, () %tuple.16, (pred[1536,1024]{0,1:T(8,128)(4,1)S(1)}, bf16[2,12,128,128]{2,3,1,0:T(8,128)(2,1)}, bf16[1024,256]{1,0:T(8,128)(2,1)}, bf16[1024,256]{1,0:T(8,128)(2,1)}) %tuple.36), branch_computations={%region_1.2_spmd, %region_2.0_spmd} | conditional | flops 1645212672 | bytes 99950664 | solution.py:76
  76.9 1.5 copy.48
  78.5 3.8 %select_reduce_fusion = (f32[2,1536]{1,0:T(2,128)S(1)}, f32[2,1536,1024]{1,2,0:T(8,128)S(1)}) fusion(pred[1536,1024]{0,1:T(8,128)(4,1)S(1)} %get-tuple-element.9, bf16[2,1536,128]{2,1,0:T(8,128)(2,1)S(1)} %bitcast.68, bf16[1024,256]{1,0:T(8,128)(2,1)} %get-tuple-element.11), kind=kOutput, calls=%fused_computation.3 | convolution fusion | flops 814740480 | bytes 15478784 | tf_op jit(solution)/shard_map/cond/branch_1_fun/kqd,pkd->kqp/dot_general | solution.py:60
  82.3 4.5 %copy-done.1 = f32[2,1536,1024]{1,2,0:T(8,128)} copy-done((f32[2,1536,1024]{1,2,0:T(8,128)}, f32[2,1536,1024]{1,2,0:T(8,128)S(1)}, u32[]{:S(2)}) %copy-start.1) | copy-done | bytes 12582936 | tf_op jit(solution)/shard_map/cond
  86.8 3.0 %fusion.1 = f32[2,1536]{1,0:T(2,128)S(1)} fusion(f32[2,1536,1024]{1,2,0:T(8,128)S(1)} %get-tuple-element.54, f32[2,1536]{1,0:T(2,128)S(1)} %broadcast_maximum_fusion, pred[1536,1024]{0,1:T(8,128)(4,1)S(1)} %get-tuple-element.9), kind=kLoop, calls=%fused_computation.5 | loop fusion | flops 12579840 | bytes 14180352 | tf_op jit(solution)/shard_map/cond/branch_1_fun/reduce_sum | solution.py:66
  89.8 7.3 %fusion.2 = f32[2,1536,128]{2,1,0:T(8,128)S(1)} fusion(f32[2,1536,1024]{1,2,0:T(8,128)} %copy-done.1, f32[2,1536]{1,0:T(2,128)S(1)} %broadcast_maximum_fusion, pred[1536,1024]{0,1:T(8,128)(4,1)S(1)} %get-tuple-element.9, bf16[1024,256]{1,0:T(8,128)(2,1)S(1)} %copy-done.2), kind=kOutput, calls=%fused_computation.6 | convolution fusion | flops 817889280 | bytes 16265216 | tf_op jit(solution)/shard_map/cond/branch_1_fun/kqp,pkd->kqd/dot_general | solution.py:67
  97.1 0.5 divide_convert_fusion
  97.6 0.4 copy.49
  98.0 1.2 copy.52
  99.2 0.6 fusion.35
  99.8 1.4 convert_reduce_fusion.1
  101.2 0.6 iota_compare_fusion.1
  103.8 0.1 dynamic-slice_reduce_fusion
  104.5 0.7 compare_select_fusion
  105.2 5.6 %scatter_custom_fusion = bf16[640,256]{1,0:T(8,128)(2,1)S(1)} fusion(s32[1024]{0:T(1024)S(1)} %compare_select_fusion, bf16[1024,256]{1,0:T(8,128)(2,1)} %all_gather.11, bf16[]{:T(256)} %constant.16.clone.1), kind=kCustom, calls=%fused_computation.31 | custom fusion | bytes 328192 | tf_op jit(solution)/shard_map/scatter | solution.py:84
  110.8 0.3 select_reduce_fusion.1
  111.1 0.9 fusion.32
  112.0 0.2 fusion.24
  112.2 0.8 dynamic-slice_convert_fusion
  112.9 5.4 %scatter_custom_fusion.1 = bf16[640,256]{1,0:T(8,128)(2,1)S(1)} fusion(s32[1024]{0:T(1024)S(1)} %compare_select_fusion, bf16[1024,256]{1,0:T(8,128)(2,1)} %all_gather.12, bf16[]{:T(256)} %constant.16.clone.1), kind=kCustom, calls=%fused_computation.29 | custom fusion | bytes 328192 | tf_op jit(solution)/shard_map/scatter | solution.py:85
  118.3 0.2 fusion.15
  118.6 30.6 %all-gather = bf16[8,1,3072]{2,1,0:T(2,128)(2,1)S(1)} all-gather(bf16[1,1,3072]{2,1,0:T(2,128)(2,1)S(1)} %reshape.110), channel_id=1, replica_groups=mesh['ctx'=8,'tp'=4] {'ctx'}, dimensions={0}, use_global_device_ids=true | all-gather | bytes 55296 | tf_op jit(solution)/shard_map/all_gather | solution.py:128
  149.1 5.0 %convolution_convert_fusion = bf16[8,1536]{1,0:T(8,128)(2,1)S(1)} fusion(bf16[3072,1536]{1,0:T(8,128)(2,1)} %param.19, bf16[8,1,3072]{2,1,0:T(2,128)(2,1)S(1)} %all-gather), kind=kOutput, calls=%fused_computation.18 | convolution fusion | flops 75509760 | bytes 9510912 | tf_op jit(solution)/shard_map/dot_general | solution.py:129
  154.1 10.9 %psum.7 = bf16[8,1536]{1,0:T(8,128)(2,1)} all-reduce(bf16[8,1536]{1,0:T(8,128)(2,1)S(1)} %convolution_convert_fusion), channel_id=1, replica_groups=mesh['ctx'=8,'tp'=4] {'tp'}, use_global_device_ids=true, to_apply=%region_13.14 | all-reduce | flops 12288 | bytes 49152 | tf_op jit(solution)/shard_map/psum | solution.py:130
  165.0 0.9 copy.53
  165.9 0.9 copy.54
  (20 shorter events, 0.1 us)
Async XLA Ops:
  0.6 7.0 %copy-start = (bf16[128,1024]{1,0:T(8,128)(2,1)S(1)}, bf16[128,1024]{1,0:T(8,128)(2,1)}, u32[]{:S(2)}) copy-start(bf16[128,1024]{1,0:T(8,128)(2,1)} %param.12) | copy-start | bytes 786436
  76.9 22.3 %copy-start.5 = (s32[4]{0:T(128)S(1)}, s32[4]{0:T(128)}, u32[]{:S(2)}) copy-start(s32[4]{0:T(128)} %param.15) | copy-start | bytes 52
  76.9 22.9 %copy-start.3 = (s32[1024]{0:T(1024)S(1)}, s32[1024]{0:T(1024)}, u32[]{:S(2)}) copy-start(s32[1024]{0:T(1024)} %param.14) | copy-start | bytes 12292
  76.9 26.9 %copy-start.4 = (bf16[4,3072]{1,0:T(4,128)(2,1)S(1)}, bf16[4,3072]{1,0:T(4,128)(2,1)}, u32[]{:S(2)}) copy-start(bf16[4,3072]{1,0:T(4,128)(2,1)} %param.16) | copy-start | bytes 73732
  82.3 4.6 %copy-start.1 = (f32[2,1536,1024]{1,2,0:T(8,128)}, f32[2,1536,1024]{1,2,0:T(8,128)S(1)}, u32[]{:S(2)}) copy-start(f32[2,1536,1024]{1,2,0:T(8,128)S(1)} %get-tuple-element.54) | copy-start | bytes 37748740 | tf_op jit(solution)/shard_map/cond
  82.3 7.5 %copy-start.2 = (bf16[1024,256]{1,0:T(8,128)(2,1)S(1)}, bf16[1024,256]{1,0:T(8,128)(2,1)}, u32[]{:S(2)}) copy-start(bf16[1024,256]{1,0:T(8,128)(2,1)} %get-tuple-element.12) | copy-start | bytes 1572868 | tf_op jit(solution)/shard_map/cond
where the time goes:
time: 167 us
  blocking collectives  110 us (66%)
  local copies, waits for them, and re-layouts  24.4 us (15%)
  matrix products  17.5 us (10%)
  other arithmetic  10.9 us (7%)
  between operations  3.98 us (2%)
    all_gather x1, blocking collectives, local(): key_piece = lax.all_gather(key_own, 'ctx', axis=0, tiled=True)  35.2 us
    all_gather x1, blocking collectives, local(): value_piece = lax.all_gather(value_own, 'ctx', axis=0, tiled=True)  33.2 us
    all_gather x1, blocking collectives, local(): gathered = lax.all_gather(decode_row, 'ctx', axis=0, tiled=True)  30.6 us
    psum x1, blocking collectives, local(): next_hidden = lax.psum(partial_value.astype(jnp.bfloat16), 'tp')  10.9 us
    dot_general x1, matrix products, update(): jnp.einsum('kqp,pkd->kqd', weights.astype(jnp.bfloat16), value_heads, pre...  7.33 us
    scatter x1, local copies, waits for them, and re-layouts, local(): cache_keys = cache_init[0].at[offset].set(place_key_piece, mode='drop')  5.57 us
    scatter x1, local copies, waits for them, and re-layouts, local(): cache_values = cache_init[1].at[offset].set(place_value_piece, mode='drop')  5.38 us
    unnamed x13, local copies, waits for them, and re-layouts  5.29 us

commit v1 on v0

v1 whole, which is shorter than its diff:
```python
import functools
import math

import jax
import jax.numpy as jnp
from jax import lax
from jax.experimental import pallas as pl
from jax.experimental.pallas import tpu as pltpu
from jax.sharding import PartitionSpec as P

H = 96
KVH = 8
HD = 128
PER = H // KVH
MESH = pl.DeviceIdType.MESH
EXP_SCALE = math.log2(math.e) / math.sqrt(HD)
F32 = jnp.float32
BF16 = jnp.bfloat16
NT = (((1,), (1,)), ((), ()))
NN = (((1,), (0,)), ((), ()))
TN = (((0,), (0,)), ((), ()))


def dot(a, b, dims):
    return lax.dot_general(a, b, dims, preferred_element_type=F32)


def kernel(
    n, ntp, heads, kv_dev,
    q_hbm, k_hbm, v_hbm, doc_ref, rep_ref, sq_ref, sk_ref, sv_ref, w_hbm,
    ctx_ref, next_ref, rk_ref, rv_ref,
    kbuf, vbuf, qbuf, wbuf, acc, tops, bias, dstart, sq_scr, sk_scr, sv_scr, att, pack, cut, out_buf, in_buf,
    local_sem, send_sem, recv_sem, part_send, part_recv,
):
    me = lax.axis_index("ctx")
    tp = lax.axis_index("tp")
    half = n // 2
    line = me // 2
    side = me % 2
    mate = 2 * line + 1 - side
    rows = kbuf.shape[1]
    width = kbuf.shape[2]
    per = heads // kv_dev
    first_kv = tp * heads // PER
    tokens = n * rows
    ndoc = sq_ref.shape[0]

    columns = pl.ds(pl.multiple_of(first_kv * HD, HD), width)
    k_copy = pltpu.make_async_copy(k_hbm.at[:, columns], kbuf.at[me], local_sem.at[0])
    v_copy = pltpu.make_async_copy(v_hbm.at[:, columns], vbuf.at[me], local_sem.at[1])
    q_copy = pltpu.make_async_copy(q_hbm, qbuf, local_sem.at[2])
    w_copy = pltpu.make_async_copy(w_hbm, wbuf, local_sem.at[3])
    k_copy.start()
    v_copy.start()
    q_copy.start()
    w_copy.start()

    barrier = pltpu.get_barrier_semaphore()
    pl.semaphore_signal(barrier, inc=1, device_id={"ctx": mate}, device_id_type=MESH)
    for t in range(1, ntp):
        pl.semaphore_signal(barrier, inc=1, device_id={"tp": lax.rem(tp + t, ntp)}, device_id_type=MESH)

    @pl.when(line > 0)
    def _():
        pl.semaphore_signal(barrier, inc=1, device_id={"ctx": me - 2}, device_id_type=MESH)

    @pl.when(line < half - 1)
    def _():
        pl.semaphore_signal(barrier, inc=1, device_id={"ctx": me + 2}, device_id_type=MESH)

    docs = doc_ref[...].astype(F32)
    starts = [jnp.sum(jnp.where(docs < d, 1.0, 0.0), axis=1, keepdims=True) for d in range(ndoc + 1)]
    own_docs = doc_ref[:, pl.ds(pl.multiple_of(me * rows, rows), rows)].astype(F32)
    begin = jnp.zeros_like(own_docs)
    for d in range(1, ndoc):
        begin = jnp.where(own_docs == d, starts[d], begin)
    dstart[...] = jnp.transpose(jnp.broadcast_to(begin, (rows, rows)))
    sq_scr[...] = jnp.zeros_like(sq_scr)
    sk_scr[...] = jnp.zeros_like(sk_scr)
    sv_scr[...] = jnp.zeros_like(sv_scr)
    sq = sq_ref[...].astype(F32)
    for h in range(heads):
        sq_scr[h, 0:ndoc, :] = sq[:, h * HD:(h + 1) * HD]
    for g in range(kv_dev):
        head_columns = pl.ds(pl.multiple_of((first_kv + g) * HD, HD), HD)
        sk_scr[g, 0:ndoc, :] = sk_ref[:, head_columns].astype(F32)
        sv_scr[g, 0:ndoc, :] = sv_ref[:, head_columns].astype(F32)
    tops[...] = jnp.full(tops.shape, -1e30, F32)
    acc[...] = jnp.zeros(acc.shape, F32)

    k_copy.wait()
    v_copy.wait()
    q_copy.wait()
    neighbours = 1 + (ntp - 1) + jnp.where(line > 0, 1, 0) + jnp.where(line < half - 1, 1, 0)
    pl.semaphore_wait(barrier, neighbours)

    def move(way, owner, piece):
        buf = (kbuf, vbuf)[piece]
        target = (me + 2, me - 2, mate)[way]
        return pltpu.make_async_remote_copy(
            src_ref=buf.at[owner],
            dst_ref=buf.at[owner],
            send_sem=send_sem.at[way, owner, piece],
            recv_sem=recv_sem.at[owner, piece],
            device_id={"ctx": target},
            device_id_type=MESH,
        )

    for piece in range(2):
        @pl.when(line < half - 1)
        def _():
            move(0, me, piece).start()

        @pl.when(line > 0)
        def _():
            move(1, me, piece).start()

        move(2, me, piece).start()

    def group(o):
        j = 2 * o * rows + lax.broadcasted_iota(jnp.int32, (rows, 2 * rows), 1)
        i = me * rows + lax.broadcasted_iota(jnp.int32, (rows, 2 * rows), 0)
        seen = (j <= i) & (j.astype(F32) >= jnp.concatenate([dstart[...]] * 2, axis=1))
        bias[...] = jnp.where(seen, 0.0, -1e30)
        for g in range(kv_dev):
            lanes = slice(g * HD, (g + 1) * HD)
            k = kbuf[pl.ds(2 * o, 2), :, lanes].reshape(2 * rows, HD)
            v = vbuf[pl.ds(2 * o, 2), :, lanes].reshape(2 * rows, HD)
            v = jnp.concatenate([v, jnp.ones_like(v)], axis=1)

            def some_heads(t, carry, g=g, k=k, v=v):
                for u in range(3):
                    h = g * per + t * 3 + u
                    q = qbuf[:, pl.ds(pl.multiple_of(h * HD, HD), HD)]
                    s = dot(q, k, NT) + bias[...]
                    old = tops[h]
                    top = jnp.maximum(old, jnp.max(s, axis=1, keepdims=True))
                    weights = jnp.exp2((s - jnp.concatenate([top, top], axis=1)) * EXP_SCALE)
                    fade = jnp.exp2((old - top) * EXP_SCALE)
                    tops[h] = top
                    acc[h] = acc[h] * jnp.concatenate([fade, fade], axis=1) + dot(weights.astype(BF16), v, NN)
                return carry

            lax.fori_loop(0, per // 3, some_heads, 0)

    back = 5 * n // 8

    def step(s, carry):
        low = line - s
        high = line + s
        for piece in range(2):
            @pl.when(low >= 0)
            def _():
                owner = 2 * low + side
                move(0, owner, piece).wait_recv()

                @pl.when(line < half - 1)
                def _():
                    move(0, owner, piece).start()

                move(2, owner, piece).start()

            @pl.when(high < half)
            def _():
                owner = 2 * high + side
                move(1, owner, piece).wait_recv()

                @pl.when(line > 0)
                def _():
                    move(1, owner, piece).start()

                move(2, owner, piece).start()
        low = line - (s - 1)
        high = line + (s - 1)

        @pl.when(low >= 0)
        def _():
            for piece in range(2):
                move(2, 2 * low + 1 - side, piece).wait_recv()

        @pl.when((high < half) & (s > 1))
        def _():
            for piece in range(2):
                move(2, 2 * high + 1 - side, piece).wait_recv()

        @pl.when((low >= 0) & (2 * low + 1 >= me - back))
        def _():
            group(low)

        return carry

    lax.fori_loop(1, half + 1, step, 0)

    shape = (per * 8, tokens)
    row_doc = (lax.broadcasted_iota(jnp.int32, shape, 0) % 8).astype(F32)
    inside = row_doc == docs
    for g in range(kv_dev):
        lanes = slice(g * HD, (g + 1) * HD)
        k = kbuf[:, :, lanes].reshape(tokens, HD)
        v = vbuf[:, :, lanes].reshape(tokens, HD)
        q = sq_scr[g * per:(g + 1) * per]
        own = jnp.sum(q * sk_scr[g][None], axis=2, keepdims=True).reshape(per * 8, 1)
        s = dot(q.reshape(per * 8, HD).astype(BF16), k, NT)
        top = jnp.maximum(jnp.max(jnp.where(inside, s, -1e30), axis=1, keepdims=True), own)
        weights = jnp.where(inside, jnp.exp2((s - top) * EXP_SCALE), 0.0)
        own_weight = jnp.exp2((own - top) * EXP_SCALE)
        total = jnp.sum(weights, axis=1, keepdims=True) + own_weight
        own_value = jnp.broadcast_to(sv_scr[g][None], (per, 8, HD)).reshape(per * 8, HD)
        mixed = dot(weights.astype(BF16), v, NN) + own_weight.astype(BF16).astype(F32) * own_value
        mixed = mixed / total
        for u in range(per):
            h = g * per + u
            att[0:8, h * HD:(h + 1) * HD] = mixed[u * 8:(u + 1) * 8]
    att[8:16, :] = jnp.zeros((8, heads * HD), F32)

    w_copy.wait()
    pieces = cut.shape[0]
    size = cut.shape[2]
    rows_in = att[...].astype(BF16)
    for c in range(pieces):
        cut[c] = dot(rows_in, wbuf[:, c * size:(c + 1) * size], NN)[0:8]
    pack[...] = jnp.zeros_like(pack)
    for c in range(pieces):
        pack[c * ndoc:(c + 1) * ndoc, :] = cut[c, 0:ndoc, :]
    out_buf[...] = pack[...].astype(BF16)
    sends = []
    for t in range(1, ntp):
        sends.append(pltpu.make_async_remote_copy(
            src_ref=out_buf,
            dst_ref=in_buf.at[t],
            send_sem=part_send.at[t],
            recv_sem=part_recv.at[t],
            device_id={"tp": lax.rem(tp + t, ntp)},
            device_id_type=MESH,
        ))
    for copy in sends:
        copy.start()

    for h in range(heads):
        ctx_ref[:, h * HD:(h + 1) * HD] = (acc[h, :, 0:HD] / acc[h, :, HD:2 * HD]).astype(BF16)

    start = jnp.zeros((1, 1), F32)
    length = jnp.zeros((1, 1), F32)
    for d in range(ndoc):
        named = rep_ref[d] == me
        start = jnp.where(named, starts[d], start)
        length = jnp.where(named, starts[d + 1] - starts[d], length)
    slots = rk_ref.shape[2]
    out_rows = rk_ref.shape[1]
    chunk = slots // max(1, tokens // 1024)
    for first in range(0, slots, chunk):
        slot = (first + lax.broadcasted_iota(jnp.int32, (1, chunk), 1)).astype(F32)
        source = jnp.where(slot < length, slot + start, -1.0)
        position = lax.broadcasted_iota(jnp.int32, (tokens, chunk), 0).astype(F32)
        pick = jnp.where(position == source, 1.0, 0.0).astype(BF16)
        for buf, ref in ((kbuf, rk_ref), (vbuf, rv_ref)):
            taken = dot(buf[...].reshape(tokens, width), pick, TN).astype(BF16)
            if out_rows < width:
                taken = jnp.where(tp % (width // out_rows) == 0, taken[0:out_rows], taken[out_rows:2 * out_rows])
            ref[0, :, first:first + chunk] = taken

    summed = out_buf[...].astype(F32)
    for t in range(1, ntp):
        sends[t - 1].wait_recv()
        summed = summed + in_buf[t].astype(F32)
    replica = lax.broadcasted_iota(jnp.int32, (n, size), 0)
    for c in range(pieces):
        result = jnp.zeros((n, size), F32)
        for d in range(ndoc):
            row = c * ndoc + d
            result = jnp.where(replica == rep_ref[d], summed[row:row + 1, :], result)
        next_ref[:, c * size:(c + 1) * size] = result.astype(BF16)
    for copy in sends:
        copy.wait_send()

    def drain(s, carry):
        for piece in range(2):
            @pl.when(line - s >= 0)
            def _():
                owner = 2 * (line - s) + side

                @pl.when(line < half - 1)
                def _():
                    move(0, owner, piece).wait_send()

                move(2, owner, piece).wait_send()

            @pl.when(line + s < half)
            def _():
                owner = 2 * (line + s) + side

                @pl.when(line > 0)
                def _():
                    move(1, owner, piece).wait_send()

                @pl.when(s > 0)
                def _():
                    move(2, owner, piece).wait_send()
        return carry

    lax.fori_loop(0, half, drain, 0)


def local(queries, keys, values, doc_ids, replica_of, step_query, step_key, step_value, out_weight):
    n = lax.axis_size("ctx")
    ntp = lax.axis_size("tp")
    rows, depth = queries.shape
    heads = depth // HD
    kv_dev = max(1, heads // PER)
    tokens = n * rows
    slots = 5 * tokens // 8
    out_columns = out_weight.shape[1]
    width = kv_dev * HD
    pieces = 4 if out_columns % 512 == 0 else 1
    size = out_columns // pieces
    vmem = pl.BlockSpec(memory_space=pltpu.VMEM)
    smem = pl.BlockSpec(memory_space=pltpu.SMEM)
    hbm = pl.BlockSpec(memory_space=pl.ANY)
    share = keys.shape[1] // ntp
    return pl.pallas_call(
        functools.partial(kernel, n, ntp, heads, kv_dev),
        out_shape=(
            jax.ShapeDtypeStruct((rows, depth), BF16),
            jax.ShapeDtypeStruct((n, out_columns), BF16),
            jax.ShapeDtypeStruct((1, share, slots), BF16),
            jax.ShapeDtypeStruct((1, share, slots), BF16),
        ),
        in_specs=[hbm, hbm, hbm, vmem, smem, vmem, vmem, vmem, hbm],
        out_specs=(vmem, vmem, vmem, vmem),
        scratch_shapes=[
            pltpu.VMEM((n, rows, width), BF16),
            pltpu.VMEM((n, rows, width), BF16),
            pltpu.VMEM((rows, depth), BF16),
            pltpu.VMEM((depth, out_columns), BF16),
            pltpu.VMEM((heads, rows, 2 * HD), F32),
            pltpu.VMEM((heads, rows, HD), F32),
            pltpu.VMEM((rows, 2 * rows), F32),
            pltpu.VMEM((rows, rows), F32),
            pltpu.VMEM((heads, 8, HD), F32),
            pltpu.VMEM((kv_dev, 8, HD), F32),
            pltpu.VMEM((kv_dev, 8, HD), F32),
            pltpu.VMEM((16, depth), F32),
            pltpu.VMEM((16, size), F32),
            pltpu.VMEM((pieces, 8, size), F32),
            pltpu.VMEM((16, size), BF16),
            pltpu.VMEM((ntp, 16, size), BF16),
            pltpu.SemaphoreType.DMA((4,)),
            pltpu.SemaphoreType.DMA((3, n, 2)),
            pltpu.SemaphoreType.DMA((n, 2)),
            pltpu.SemaphoreType.DMA((ntp,)),
            pltpu.SemaphoreType.DMA((ntp,)),
        ],
        compiler_params=pltpu.CompilerParams(
            collective_id=0, has_side_effects=True, vmem_limit_bytes=48 * 1024 * 1024
        ),
    )(queries, keys, values, doc_ids.reshape(1, tokens), replica_of, step_query, step_key, step_value, out_weight)


def solution(mesh):
    placed = (
        P("ctx", "tp"),
        P("ctx", None),
        P("ctx", None),
        P(),
        P(),
        P(None, "tp"),
        P(),
        P(),
        P("tp", "ctx"),
    )
    return jax.shard_map(
        local,
        mesh=mesh,
        in_specs=placed,
        out_specs=(P("ctx", "tp"), P(None, "ctx"), P("ctx", "tp", None), P("ctx", "tp", None)),
        check_vma=False,
    )
```

time: 167 us -> 40 us (0.24)
  the two profiles are of different devices: /device:TPU:0 before, /device:TPU:25 now
where the time goes in v1:
time: 40 us; the launch traced here: 39.6 us
  Pallas kernels  29.5 us (74%)
  local copies, waits for them, and re-layouts  9.43 us (24%)
  between operations  0.66 us (2%)
    pallas_call x1, Pallas kernels, local(): pl.pallas_call(functools.partial(kernel, n, ntp, heads, kv_dev), out_shap...  29.5 us
    unnamed x20, local copies, waits for them, and re-layouts  9.43 us

profile of v1, /device:TPU:25, one launch (start us, length us, event | category | flops | bytes accessed | tf_op | source)
XLA Modules:
  0.0 39.6 jit_solution(15592672043833863619)
XLA Ops:
  0.6 0.0 copy-start
  0.6 1.1 %copy-done = bf16[128,3072]{1,0:T(8,128)(2,1)S(1)} copy-done((bf16[128,3072]{1,0:T(8,128)(2,1)S(1)}, bf16[128,3072]{1,0:T(8,128)(2,1)}, u32[]{:S(2)}) %copy-start) | copy-done | bytes 786456
  1.8 0.0 copy-start.1
  1.8 0.9 %copy-done.1 = bf16[128,1024]{1,0:T(8,128)(2,1)S(1)} copy-done((bf16[128,1024]{1,0:T(8,128)(2,1)S(1)}, bf16[128,1024]{1,0:T(8,128)(2,1)}, u32[]{:S(2)}) %copy-start.1) | copy-done | bytes 262168
  2.7 0.0 copy-start.2
  2.7 0.9 %copy-done.2 = bf16[128,1024]{1,0:T(8,128)(2,1)S(1)} copy-done((bf16[128,1024]{1,0:T(8,128)(2,1)S(1)}, bf16[128,1024]{1,0:T(8,128)(2,1)}, u32[]{:S(2)}) %copy-start.2) | copy-done | bytes 262168
  3.7 0.0 copy-start.3
  3.7 0.7 %copy-done.3 = bf16[4,3072]{1,0:T(4,128)(2,1)S(1)} copy-done((bf16[4,3072]{1,0:T(4,128)(2,1)S(1)}, bf16[4,3072]{1,0:T(4,128)(2,1)}, u32[]{:S(2)}) %copy-start.3) | copy-done | bytes 24600
  4.4 0.0 copy-start.4
  4.4 0.7 %copy-done.4 = bf16[4,1024]{1,0:T(4,128)(2,1)S(1)} copy-done((bf16[4,1024]{1,0:T(4,128)(2,1)S(1)}, bf16[4,1024]{1,0:T(4,128)(2,1)}, u32[]{:S(2)}) %copy-start.4) | copy-done | bytes 8216
  5.1 0.0 copy-start.5
  5.1 0.7 %copy-done.5 = bf16[4,1024]{1,0:T(4,128)(2,1)S(1)} copy-done((bf16[4,1024]{1,0:T(4,128)(2,1)S(1)}, bf16[4,1024]{1,0:T(4,128)(2,1)}, u32[]{:S(2)}) %copy-start.5) | copy-done | bytes 8216
  5.8 0.0 copy-start.6
  5.8 0.7 %copy-done.6 = s32[1024]{0:T(1024)S(1)} copy-done((s32[1024]{0:T(1024)S(1)}, s32[1024]{0:T(1024)}, u32[]{:S(2)}) %copy-start.6) | copy-done | bytes 4120
  6.5 0.0 copy-start.7
  6.5 0.7 %copy-done.7 = s32[4]{0:T(128)S(1)} copy-done((s32[4]{0:T(128)S(1)}, s32[4]{0:T(128)}, u32[]{:S(2)}) %copy-start.7) | copy-done | bytes 40
  7.1 29.5 %shard_map.120 = (bf16[128,3072]{1,0:T(8,128)(2,1)S(1)}, bf16[8,1536]{1,0:T(8,128)(2,1)S(1)}, bf16[1,256,640]{2,1,0:T(8,128)(2,1)S(1)}, bf16[1,256,640]{2,1,0:T(8,128)(2,1)S(1)}) custom-call(bf16[128,3072]{1,0:T(8,128)(2,1)S(1)} %copy-done, bf16[128,1024]{1,0:T(8,128)(2,1)S(1)} %copy-done.1, bf16[128,1024]{1,0:T(8,128)(2,1)S(1)} %copy-done.2, ...), custom_call_target="tpu_custom_call" | custom-call | tf_op jit(solution)/shard_map/pallas_call | solution.py:320
  36.6 0.9 %copy.17 = bf16[128,3072]{1,0:T(8,128)(2,1)} copy(bf16[128,3072]{1,0:T(8,128)(2,1)S(1)} %get-tuple-element.8) | data formatting | bytes 1572864
  37.5 0.6 %copy.18 = bf16[8,1536]{1,0:T(8,128)(2,1)} copy(bf16[8,1536]{1,0:T(8,128)(2,1)S(1)} %get-tuple-element.9) | data formatting | bytes 49152
  38.1 0.7 %copy.19 = bf16[1,256,640]{2,1,0:T(8,128)(2,1)} copy(bf16[1,256,640]{2,1,0:T(8,128)(2,1)S(1)} %get-tuple-element.10) | data formatting | bytes 655360
  38.9 0.7 %copy.20 = bf16[1,256,640]{2,1,0:T(8,128)(2,1)} copy(bf16[1,256,640]{2,1,0:T(8,128)(2,1)S(1)} %get-tuple-element.11) | data formatting | bytes 655360
Async XLA Ops:
  0.6 1.1 %copy-start = (bf16[128,3072]{1,0:T(8,128)(2,1)S(1)}, bf16[128,3072]{1,0:T(8,128)(2,1)}, u32[]{:S(2)}) copy-start(bf16[128,3072]{1,0:T(8,128)(2,1)} %q_hbm.1) | copy-start | bytes 2359300
  1.8 0.9 %copy-start.1 = (bf16[128,1024]{1,0:T(8,128)(2,1)S(1)}, bf16[128,1024]{1,0:T(8,128)(2,1)}, u32[]{:S(2)}) copy-start(bf16[128,1024]{1,0:T(8,128)(2,1)} %k_hbm.1) | copy-start | bytes 786436
  2.7 0.9 %copy-start.2 = (bf16[128,1024]{1,0:T(8,128)(2,1)S(1)}, bf16[128,1024]{1,0:T(8,128)(2,1)}, u32[]{:S(2)}) copy-start(bf16[128,1024]{1,0:T(8,128)(2,1)} %v_hbm.1) | copy-start | bytes 786436
  3.7 0.7 %copy-start.3 = (bf16[4,3072]{1,0:T(4,128)(2,1)S(1)}, bf16[4,3072]{1,0:T(4,128)(2,1)}, u32[]{:S(2)}) copy-start(bf16[4,3072]{1,0:T(4,128)(2,1)} %sq_ref.1) | copy-start | bytes 73732
  4.4 0.7 %copy-start.4 = (bf16[4,1024]{1,0:T(4,128)(2,1)S(1)}, bf16[4,1024]{1,0:T(4,128)(2,1)}, u32[]{:S(2)}) copy-start(bf16[4,1024]{1,0:T(4,128)(2,1)} %sk_ref.1) | copy-start | bytes 24580
  5.1 0.7 %copy-start.5 = (bf16[4,1024]{1,0:T(4,128)(2,1)S(1)}, bf16[4,1024]{1,0:T(4,128)(2,1)}, u32[]{:S(2)}) copy-start(bf16[4,1024]{1,0:T(4,128)(2,1)} %sv_ref.1) | copy-start | bytes 24580
  5.8 0.7 %copy-start.6 = (s32[1024]{0:T(1024)S(1)}, s32[1024]{0:T(1024)}, u32[]{:S(2)}) copy-start(s32[1024]{0:T(1024)} %param.12) | copy-start | bytes 12292
  6.5 0.7 %copy-start.7 = (s32[4]{0:T(128)S(1)}, s32[4]{0:T(128)}, u32[]{:S(2)}) copy-start(s32[4]{0:T(128)} %rep_ref.1) | copy-start | bytes 52

commit v2 on v1

--- a/solution.py
+++ b/solution.py
@@ -27,10 +27,10 @@
 
 def kernel(
     n, ntp, heads, kv_dev,
-    q_hbm, k_hbm, v_hbm, doc_ref, rep_ref, sq_ref, sk_ref, sv_ref, w_hbm,
+    q_hbm, k_hbm, v_hbm, doc_hbm, rep_hbm, sq_hbm, sk_hbm, sv_hbm, w_hbm,
     ctx_ref, next_ref, rk_ref, rv_ref,
     kbuf, vbuf, qbuf, wbuf, acc, tops, bias, dstart, sq_scr, sk_scr, sv_scr, att, pack, cut, out_buf, in_buf,
-    local_sem, send_sem, recv_sem, part_send, part_recv,
+    doc_ref, rep_ref, sq_ref, sk_ref, sv_ref, local_sem, send_sem, recv_sem, part_send, part_recv,
 ):
     me = lax.axis_index("ctx")
     tp = lax.axis_index("tp")
@@ -52,6 +52,14 @@
     w_copy = pltpu.make_async_copy(w_hbm, wbuf, local_sem.at[3])
     k_copy.start()
     v_copy.start()
+    small = [
+        pltpu.make_async_copy(src, dst, local_sem.at[4 + i])
+        for i, (src, dst) in enumerate((
+            (doc_hbm, doc_ref), (rep_hbm, rep_ref), (sq_hbm, sq_ref), (sk_hbm, sk_ref), (sv_hbm, sv_ref),
+        ))
+    ]
+    for copy in small:
+        copy.start()
     q_copy.start()
     w_copy.start()
 
@@ -68,6 +76,8 @@
     def _():
         pl.semaphore_signal(barrier, inc=1, device_id={"ctx": me + 2}, device_id_type=MESH)
 
+    for copy in small:
+        copy.wait()
     docs = doc_ref[...].astype(F32)
     starts = [jnp.sum(jnp.where(docs < d, 1.0, 0.0), axis=1, keepdims=True) for d in range(ndoc + 1)]
     own_docs = doc_ref[:, pl.ds(pl.multiple_of(me * rows, rows), rows)].astype(F32)
@@ -128,20 +138,20 @@
             v = vbuf[pl.ds(2 * o, 2), :, lanes].reshape(2 * rows, HD)
             v = jnp.concatenate([v, jnp.ones_like(v)], axis=1)
 
-            def some_heads(t, carry, g=g, k=k, v=v):
-                for u in range(3):
-                    h = g * per + t * 3 + u
-                    q = qbuf[:, pl.ds(pl.multiple_of(h * HD, HD), HD)]
-                    s = dot(q, k, NT) + bias[...]
-                    old = tops[h]
-                    top = jnp.maximum(old, jnp.max(s, axis=1, keepdims=True))
-                    weights = jnp.exp2((s - jnp.concatenate([top, top], axis=1)) * EXP_SCALE)
-                    fade = jnp.exp2((old - top) * EXP_SCALE)
-                    tops[h] = top
-                    acc[h] = acc[h] * jnp.concatenate([fade, fade], axis=1) + dot(weights.astype(BF16), v, NN)
-                return carry
-
-            lax.fori_loop(0, per // 3, some_heads, 0)
+            q = jnp.concatenate(
+                [qbuf[:, (g * per + u) * HD:(g * per + u + 1) * HD] for u in range(per)], axis=0
+            )
+            s = dot(q, k, NT).reshape(per, rows, 2 * rows) + bias[...][None]
+            old = tops[g * per:(g + 1) * per]
+            top = jnp.maximum(old, jnp.max(s, axis=2, keepdims=True))
+            weights = jnp.exp2((s - jnp.concatenate([top, top], axis=2)) * EXP_SCALE)
+            fade = jnp.exp2((old - top) * EXP_SCALE)
+            tops[g * per:(g + 1) * per] = top
+            new = dot(weights.reshape(per * rows, 2 * rows).astype(BF16), v, NN)
+            acc[g * per:(g + 1) * per] = (
+                acc[g * per:(g + 1) * per] * jnp.concatenate([fade, fade], axis=2)
+                + new.reshape(per, rows, 2 * HD)
+            )
 
     back = 5 * n // 8
 
@@ -314,7 +324,6 @@
     pieces = 4 if out_columns % 512 == 0 else 1
     size = out_columns // pieces
     vmem = pl.BlockSpec(memory_space=pltpu.VMEM)
-    smem = pl.BlockSpec(memory_space=pltpu.SMEM)
     hbm = pl.BlockSpec(memory_space=pl.ANY)
     share = keys.shape[1] // ntp
     return pl.pallas_call(
@@ -325,7 +334,7 @@
             jax.ShapeDtypeStruct((1, share, slots), BF16),
             jax.ShapeDtypeStruct((1, share, slots), BF16),
         ),
-        in_specs=[hbm, hbm, hbm, vmem, smem, vmem, vmem, vmem, hbm],
+        in_specs=[hbm] * 9,
         out_specs=(vmem, vmem, vmem, vmem),
         scratch_shapes=[
             pltpu.VMEM((n, rows, width), BF16),
@@ -344,14 +353,19 @@
             pltpu.VMEM((pieces, 8, size), F32),
             pltpu.VMEM((16, size), BF16),
             pltpu.VMEM((ntp, 16, size), BF16),
-            pltpu.SemaphoreType.DMA((4,)),
+            pltpu.VMEM((1, tokens), jnp.int32),
+            pltpu.SMEM(replica_of.shape, jnp.int32),
+            pltpu.VMEM(step_query.shape, BF16),
+            pltpu.VMEM(step_key.shape, BF16),
+            pltpu.VMEM(step_value.shape, BF16),
+            pltpu.SemaphoreType.DMA((9,)),
             pltpu.SemaphoreType.DMA((3, n, 2)),
             pltpu.SemaphoreType.DMA((n, 2)),
             pltpu.SemaphoreType.DMA((ntp,)),
             pltpu.SemaphoreType.DMA((ntp,)),
         ],
         compiler_params=pltpu.CompilerParams(
-            collective_id=0, has_side_effects=True, vmem_limit_bytes=48 * 1024 * 1024
+            collective_id=0, has_side_effects=True, vmem_limit_bytes=60 * 1024 * 1024
         ),
     )(queries, keys, values, doc_ids.reshape(1, tokens), replica_of, step_query, step_key, step_value, out_weight)
 

time: 40 us -> 34.4 us (0.86)
  the two profiles are of different devices: /device:TPU:25 before, /device:TPU:0 now
where the time goes in v2:
time: 34.4 us; the launch traced here: 34.2 us
  Pallas kernels  26.7 us (78%)
  local copies, waits for them, and re-layouts  6.86 us (20%)
  between operations  0.64 us (2%)
    pallas_call x1, Pallas kernels, local(): pl.pallas_call(functools.partial(kernel, n, ntp, heads, kv_dev), out_shap...  26.7 us
    unnamed x4, local copies, waits for them, and re-layouts  6.86 us

profile of v2, /device:TPU:0, one launch (start us, length us, event | category | flops | bytes accessed | tf_op | source)
XLA Modules:
  0.0 34.2 jit_solution(11223194212140881976)
XLA Ops:
  0.6 26.7 %shard_map.120 = (bf16[128,3072]{1,0:T(8,128)(2,1)}, bf16[8,1536]{1,0:T(8,128)(2,1)}, bf16[1,256,640]{2,1,0:T(8,128)(2,1)}, bf16[1,256,640]{2,1,0:T(8,128)(2,1)}) custom-call(bf16[128,3072]{1,0:T(8,128)(2,1)} %q_hbm.1, bf16[128,1024]{1,0:T(8,128)(2,1)} %k_hbm.1, bf16[128,1024]{1,0:T(8,128)(2,1)} %v_hbm.1, s32[1,1024]{1,0:T(1,128)} %bitcast.1, s32[4]{0:T(128)} %rep_hbm.1, ...), custom_call_target="tpu_custom_call" | custom-call | tf_op jit(solution)/shard_map/pallas_call | solution.py:329
  27.3 2.1 %copy.17 = bf16[128,3072]{1,0:T(8,128)(2,1)} copy(bf16[128,3072]{1,0:T(8,128)(2,1)} %get-tuple-element.8) | data formatting | bytes 1572864
  29.4 1.3 %copy.18 = bf16[8,1536]{1,0:T(8,128)(2,1)} copy(bf16[8,1536]{1,0:T(8,128)(2,1)} %get-tuple-element.9) | data formatting | bytes 49152
  30.7 1.7 %copy.19 = bf16[1,256,640]{2,1,0:T(8,128)(2,1)} copy(bf16[1,256,640]{2,1,0:T(8,128)(2,1)} %get-tuple-element.10) | data formatting | bytes 655360
  32.4 1.7 %copy.20 = bf16[1,256,640]{2,1,0:T(8,128)(2,1)} copy(bf16[1,256,640]{2,1,0:T(8,128)(2,1)} %get-tuple-element.11) | data formatting | bytes 655360

commit v3 on v2

--- a/solution.py
+++ b/solution.py
@@ -26,11 +26,12 @@
 
 
 def kernel(
-    n, ntp, heads, kv_dev,
+    n, ntp, heads, kv_dev, combiners,
     q_hbm, k_hbm, v_hbm, doc_hbm, rep_hbm, sq_hbm, sk_hbm, sv_hbm, w_hbm,
-    ctx_ref, next_ref, rk_ref, rv_ref,
+    ctx_hbm, next_hbm, rk_hbm, rv_hbm,
     kbuf, vbuf, qbuf, wbuf, acc, tops, bias, dstart, sq_scr, sk_scr, sv_scr, att, pack, cut, out_buf, in_buf,
-    doc_ref, rep_ref, sq_ref, sk_ref, sv_ref, local_sem, send_sem, recv_sem, part_send, part_recv,
+    part, comb, mixed, ctx_ref, next_ref, rk_ref, rv_ref, out_sem,
+    doc_ref, rep_ref, sq_ref, sk_ref, sv_ref, local_sem, send_sem, recv_sem, part_send, part_recv, comb_send, comb_recv, mix_send, mix_recv,
 ):
     me = lax.axis_index("ctx")
     tp = lax.axis_index("tp")
@@ -43,6 +44,8 @@
     per = heads // kv_dev
     first_kv = tp * heads // PER
     tokens = n * rows
+    pieces = cut.shape[0]
+    size = cut.shape[2]
     ndoc = sq_ref.shape[0]
 
     columns = pl.ds(pl.multiple_of(first_kv * HD, HD), width)
@@ -64,17 +67,10 @@
     w_copy.start()
 
     barrier = pltpu.get_barrier_semaphore()
-    pl.semaphore_signal(barrier, inc=1, device_id={"ctx": mate}, device_id_type=MESH)
+    for t in range(1, n):
+        pl.semaphore_signal(barrier, inc=1, device_id={"ctx": lax.rem(me + t, n)}, device_id_type=MESH)
     for t in range(1, ntp):
         pl.semaphore_signal(barrier, inc=1, device_id={"tp": lax.rem(tp + t, ntp)}, device_id_type=MESH)
-
-    @pl.when(line > 0)
-    def _():
-        pl.semaphore_signal(barrier, inc=1, device_id={"ctx": me - 2}, device_id_type=MESH)
-
-    @pl.when(line < half - 1)
-    def _():
-        pl.semaphore_signal(barrier, inc=1, device_id={"ctx": me + 2}, device_id_type=MESH)
 
     for copy in small:
         copy.wait()
@@ -90,19 +86,21 @@
     sv_scr[...] = jnp.zeros_like(sv_scr)
     sq = sq_ref[...].astype(F32)
     for h in range(heads):
-        sq_scr[h, 0:ndoc, :] = sq[:, h * HD:(h + 1) * HD]
+        low = h % 2 * ndoc
+        sq_scr[h // 2, low:low + ndoc, :] = sq[:, h * HD:(h + 1) * HD]
     for g in range(kv_dev):
         head_columns = pl.ds(pl.multiple_of((first_kv + g) * HD, HD), HD)
-        sk_scr[g, 0:ndoc, :] = sk_ref[:, head_columns].astype(F32)
-        sv_scr[g, 0:ndoc, :] = sv_ref[:, head_columns].astype(F32)
+        for low in (0, ndoc):
+            sk_scr[g, low:low + ndoc, :] = sk_ref[:, head_columns].astype(F32)
+            sv_scr[g, low:low + ndoc, :] = sv_ref[:, head_columns].astype(F32)
+    att[...] = jnp.zeros(att.shape, F32)
     tops[...] = jnp.full(tops.shape, -1e30, F32)
     acc[...] = jnp.zeros(acc.shape, F32)
 
     k_copy.wait()
     v_copy.wait()
     q_copy.wait()
-    neighbours = 1 + (ntp - 1) + jnp.where(line > 0, 1, 0) + jnp.where(line < half - 1, 1, 0)
-    pl.semaphore_wait(barrier, neighbours)
+    pl.semaphore_wait(barrier, (n - 1) + (ntp - 1))
 
     def move(way, owner, piece):
         buf = (kbuf, vbuf)[piece]
@@ -126,6 +124,112 @@
             move(1, me, piece).start()
 
         move(2, me, piece).start()
+
+    pairs = heads // 2
+    group_pairs = pairs // kv_dev
+    share = pairs // combiners
+    shape = (group_pairs * 8, rows)
+    row_doc = (lax.broadcasted_iota(jnp.int32, shape, 0) % ndoc).astype(F32)
+    inside = row_doc == own_docs
+    for g in range(kv_dev):
+        lanes = slice(g * HD, (g + 1) * HD)
+        q = sq_scr[g * group_pairs:(g + 1) * group_pairs].reshape(group_pairs * 8, HD).astype(BF16)
+        s = dot(q, kbuf[me, :, lanes], NT)
+        top = jnp.max(jnp.where(inside, s, -1e30), axis=1, keepdims=True)
+        weights = jnp.where(inside, jnp.exp2((s - top) * EXP_SCALE), 0.0)
+        total = jnp.sum(weights, axis=1, keepdims=True)
+        summed = dot(weights.astype(BF16), vbuf[me, :, lanes], NN)
+        half_lane = lax.broadcasted_iota(jnp.int32, (group_pairs * 8, HD), 1) < HD // 2
+        both = jnp.concatenate([summed, jnp.where(half_lane, top, total)], axis=1)
+        part[g * group_pairs:(g + 1) * group_pairs] = both.reshape(group_pairs, 8, 2 * HD)
+
+    def to_combiner(t):
+        target = lax.rem(me + t, n)
+        return pltpu.make_async_remote_copy(
+            src_ref=part.at[pl.ds(jnp.minimum(target, combiners - 1) * share, share)],
+            dst_ref=comb.at[me],
+            send_sem=comb_send.at[t],
+            recv_sem=comb_recv.at[me],
+            device_id={"ctx": target},
+            device_id_type=MESH,
+        )
+
+    def from_device(sender):
+        return pltpu.make_async_remote_copy(
+            src_ref=comb.at[sender],
+            dst_ref=comb.at[sender],
+            send_sem=comb_send.at[0],
+            recv_sem=comb_recv.at[sender],
+            device_id={"ctx": mate},
+            device_id_type=MESH,
+        )
+
+    def mix_copy(t, slot):
+        return pltpu.make_async_remote_copy(
+            src_ref=mixed.at[slot],
+            dst_ref=mixed.at[slot],
+            send_sem=mix_send.at[t],
+            recv_sem=mix_recv.at[slot],
+            device_id={"ctx": lax.rem(me + t, n)},
+            device_id_type=MESH,
+        )
+
+    for t in range(1, n):
+        @pl.when(lax.rem(me + t, n) < combiners)
+        def _():
+            to_combiner(t).start()
+
+    def combine():
+        comb[me] = part[pl.ds(me * share, share)]
+        for t in range(1, n):
+            from_device(lax.rem(me + t, n)).wait_recv()
+        for j in range(share):
+            pair = me * share + j
+            g = pair // group_pairs
+            own = jnp.sum(sq_scr[pair] * sk_scr[g], axis=1, keepdims=True)
+            top = own
+            for i in range(n):
+                top = jnp.maximum(top, comb[i, j, :, HD:HD + 1])
+            own_weight = jnp.exp2((own - top) * EXP_SCALE)
+            total = own_weight
+            summed = own_weight.astype(BF16).astype(F32) * sv_scr[g]
+            for i in range(n):
+                fade = jnp.exp2((comb[i, j, :, HD:HD + 1] - top) * EXP_SCALE)
+                total = total + fade * comb[i, j, :, HD + HD // 2:HD + HD // 2 + 1]
+                summed = summed + fade * comb[i, j, :, 0:HD]
+            mixed[me, j] = summed / total
+        for t in range(1, n):
+            mix_copy(t, me).start()
+
+    def project():
+        for c in range(combiners):
+            @pl.when(c != me)
+            def _():
+                mix_copy(1, c).wait_recv()
+        for h in range(heads):
+            low = h % 2 * ndoc
+            pair = h // 2
+            att[0:ndoc, h * HD:(h + 1) * HD] = mixed[pair // share, pair % share, low:low + ndoc, :]
+        w_copy.wait()
+        rows_in = att[...].astype(BF16)
+        for c in range(pieces):
+            cut[c] = dot(rows_in, wbuf[:, c * size:(c + 1) * size], NN)[0:8]
+        pack[...] = jnp.zeros_like(pack)
+        for c in range(pieces):
+            pack[c * ndoc:(c + 1) * ndoc, :] = cut[c, 0:ndoc, :]
+        out_buf[...] = pack[...].astype(BF16)
+        for t in range(1, ntp):
+            term(t).start()
+
+    def term(t):
+        return pltpu.make_async_remote_copy(
+            src_ref=out_buf,
+            dst_ref=in_buf.at[t],
+            send_sem=part_send.at[t],
+            recv_sem=part_recv.at[t],
+            device_id={"tp": lax.rem(tp + t, ntp)},
+            device_id_type=MESH,
+        )
 
     def group(o):
         j = 2 * o * rows + lax.broadcasted_iota(jnp.int32, (rows, 2 * rows), 1)
@@ -180,6 +284,10 @@
                     move(1, owner, piece).start()
 
                 move(2, owner, piece).start()
+        @pl.when(s == half - 1)
+        def _():
+            project()
+
         low = line - (s - 1)
         high = line + (s - 1)
 
@@ -197,57 +305,24 @@
         def _():
             group(low)
 
+        @pl.when((s == 1) & (me < combiners))
+        def _():
+            combine()
+
         return carry
 
     lax.fori_loop(1, half + 1, step, 0)
-
-    shape = (per * 8, tokens)
-    row_doc = (lax.broadcasted_iota(jnp.int32, shape, 0) % 8).astype(F32)
-    inside = row_doc == docs
-    for g in range(kv_dev):
-        lanes = slice(g * HD, (g + 1) * HD)
-        k = kbuf[:, :, lanes].reshape(tokens, HD)
-        v = vbuf[:, :, lanes].reshape(tokens, HD)
-        q = sq_scr[g * per:(g + 1) * per]
-        own = jnp.sum(q * sk_scr[g][None], axis=2, keepdims=True).reshape(per * 8, 1)
-        s = dot(q.reshape(per * 8, HD).astype(BF16), k, NT)
-        top = jnp.maximum(jnp.max(jnp.where(inside, s, -1e30), axis=1, keepdims=True), own)
-        weights = jnp.where(inside, jnp.exp2((s - top) * EXP_SCALE), 0.0)
-        own_weight = jnp.exp2((own - top) * EXP_SCALE)
-        total = jnp.sum(weights, axis=1, keepdims=True) + own_weight
-        own_value = jnp.broadcast_to(sv_scr[g][None], (per, 8, HD)).reshape(per * 8, HD)
-        mixed = dot(weights.astype(BF16), v, NN) + own_weight.astype(BF16).astype(F32) * own_value
-        mixed = mixed / total
-        for u in range(per):
-            h = g * per + u
-            att[0:8, h * HD:(h + 1) * HD] = mixed[u * 8:(u + 1) * 8]
-    att[8:16, :] = jnp.zeros((8, heads * HD), F32)
-
-    w_copy.wait()
-    pieces = cut.shape[0]
-    size = cut.shape[2]
-    rows_in = att[...].astype(BF16)
-    for c in range(pieces):
-        cut[c] = dot(rows_in, wbuf[:, c * size:(c + 1) * size], NN)[0:8]
-    pack[...] = jnp.zeros_like(pack)
-    for c in range(pieces):
-        pack[c * ndoc:(c + 1) * ndoc, :] = cut[c, 0:ndoc, :]
-    out_buf[...] = pack[...].astype(BF16)
-    sends = []
-    for t in range(1, ntp):
-        sends.append(pltpu.make_async_remote_copy(
-            src_ref=out_buf,
-            dst_ref=in_buf.at[t],
-            send_sem=part_send.at[t],
-            recv_sem=part_recv.at[t],
-            device_id={"tp": lax.rem(tp + t, ntp)},
-            device_id_type=MESH,
-        ))
-    for copy in sends:
-        copy.start()
 
     for h in range(heads):
         ctx_ref[:, h * HD:(h + 1) * HD] = (acc[h, :, 0:HD] / acc[h, :, HD:2 * HD]).astype(BF16)
+
+    results = [
+        pltpu.make_async_copy(src, dst, out_sem.at[i])
+        for i, (src, dst) in enumerate((
+            (ctx_ref, ctx_hbm), (rk_ref, rk_hbm), (rv_ref, rv_hbm), (next_ref, next_hbm),
+        ))
+    ]
+    results[0].start()
 
     start = jnp.zeros((1, 1), F32)
     length = jnp.zeros((1, 1), F32)
@@ -269,9 +344,12 @@
                 taken = jnp.where(tp % (width // out_rows) == 0, taken[0:out_rows], taken[out_rows:2 * out_rows])
             ref[0, :, first:first + chunk] = taken
 
+    results[1].start()
+    results[2].start()
+
     summed = out_buf[...].astype(F32)
     for t in range(1, ntp):
-        sends[t - 1].wait_recv()
+        term(t).wait_recv()
         summed = summed + in_buf[t].astype(F32)
     replica = lax.broadcasted_iota(jnp.int32, (n, size), 0)
     for c in range(pieces):
@@ -280,8 +358,17 @@
             row = c * ndoc + d
             result = jnp.where(replica == rep_ref[d], summed[row:row + 1, :], result)
         next_ref[:, c * size:(c + 1) * size] = result.astype(BF16)
-    for copy in sends:
-        copy.wait_send()
+    results[3].start()
+    for t in range(1, ntp):
+        term(t).wait_send()
+    for t in range(1, n):
+        @pl.when(lax.rem(me + t, n) < combiners)
+        def _():
+            to_combiner(t).wait_send()
+
+        @pl.when(me < combiners)
+        def _():
+            mix_copy(t, me).wait_send()
 
     def drain(s, carry):
         for piece in range(2):
@@ -309,6 +396,16 @@
         return carry
 
     lax.fori_loop(0, half, drain, 0)
+    for copy in results:
+        copy.wait()
+
+
+def deliver(*refs):
+    copies = [pltpu.make_async_copy(refs[i], refs[4 + i], refs[8].at[i]) for i in range(4)]
+    for copy in copies:
+        copy.start()
+    for copy in copies:
+        copy.wait()
 
 
 def local(queries, keys, values, doc_ids, replica_of, step_query, step_key, step_value, out_weight):
@@ -323,11 +420,12 @@
     width = kv_dev * HD
     pieces = 4 if out_columns % 512 == 0 else 1
     size = out_columns // pieces
-    vmem = pl.BlockSpec(memory_space=pltpu.VMEM)
     hbm = pl.BlockSpec(memory_space=pl.ANY)
     share = keys.shape[1] // ntp
-    return pl.pallas_call(
-        functools.partial(kernel, n, ntp, heads, kv_dev),
+    pairs = heads // 2
+    combiners = max(c for c in range(1, n + 1) if pairs % c == 0)
+    results = pl.pallas_call(
+        functools.partial(kernel, n, ntp, heads, kv_dev, combiners),
         out_shape=(
             jax.ShapeDtypeStruct((rows, depth), BF16),
             jax.ShapeDtypeStruct((n, out_columns), BF16),
@@ -335,7 +433,7 @@
             jax.ShapeDtypeStruct((1, share, slots), BF16),
         ),
         in_specs=[hbm] * 9,
-        out_specs=(vmem, vmem, vmem, vmem),
+        out_specs=(hbm,) * 4,
         scratch_shapes=[
             pltpu.VMEM((n, rows, width), BF16),
             pltpu.VMEM((n, rows, width), BF16),
@@ -345,7 +443,7 @@
             pltpu.VMEM((heads, rows, HD), F32),
             pltpu.VMEM((rows, 2 * rows), F32),
             pltpu.VMEM((rows, rows), F32),
-            pltpu.VMEM((heads, 8, HD), F32),
+            pltpu.VMEM((pairs, 8, HD), F32),
             pltpu.VMEM((kv_dev, 8, HD), F32),
             pltpu.VMEM((kv_dev, 8, HD), F32),
             pltpu.VMEM((16, depth), F32),
@@ -353,6 +451,14 @@
             pltpu.VMEM((pieces, 8, size), F32),
             pltpu.VMEM((16, size), BF16),
             pltpu.VMEM((ntp, 16, size), BF16),
+            pltpu.VMEM((pairs, 8, 2 * HD), F32),
+            pltpu.VMEM((n, pairs // combiners, 8, 2 * HD), F32),
+            pltpu.VMEM((combiners, pairs // combiners, 8, HD), F32),
+            pltpu.VMEM((rows, depth), BF16),
+            pltpu.VMEM((n, out_columns), BF16),
+            pltpu.VMEM((1, share, slots), BF16),
+            pltpu.VMEM((1, share, slots), BF16),
+            pltpu.SemaphoreType.DMA((4,)),
             pltpu.VMEM((1, tokens), jnp.int32),
             pltpu.SMEM(replica_of.shape, jnp.int32),
             pltpu.VMEM(step_query.shape, BF16),
@@ -363,11 +469,23 @@
             pltpu.SemaphoreType.DMA((n, 2)),
             pltpu.SemaphoreType.DMA((ntp,)),
             pltpu.SemaphoreType.DMA((ntp,)),
+            pltpu.SemaphoreType.DMA((n,)),
+            pltpu.SemaphoreType.DMA((n,)),
+            pltpu.SemaphoreType.DMA((n,)),
+            pltpu.SemaphoreType.DMA((n,)),
         ],
         compiler_params=pltpu.CompilerParams(
             collective_id=0, has_side_effects=True, vmem_limit_bytes=60 * 1024 * 1024
         ),
     )(queries, keys, values, doc_ids.reshape(1, tokens), replica_of, step_query, step_key, step_value, out_weight)
+    return pl.pallas_call(
+        deliver,
+        out_shape=tuple(jax.ShapeDtypeStruct(r.shape, r.dtype) for r in results),
+        in_specs=[hbm] * 4,
+        out_specs=(hbm,) * 4,
+        scratch_shapes=[pltpu.SemaphoreType.DMA((4,))],
+        compiler_params=pltpu.CompilerParams(vmem_limit_bytes=60 * 1024 * 1024),
+    )(*results)
 
 
 def solution(mesh):

time: 34.4 us -> 71.8 us (2.09)
  Pallas kernels: 26.7 us -> 71 us
  local copies, waits for them, and re-layouts: 6.86 us -> 0 us
    pallas_call x1 -> x2, Pallas kernels: 26.7 us -> 71 us  [the longest x1 45.6 us: local(): pl.pallas_call(deliver, out_shape=tuple((jax.ShapeDtypeStruct(r.shape, r....]
    unnamed x4 -> x0, local copies, waits for them, and re-layouts: 6.86 us -> none
where the time goes in v3:
time: 71.8 us; the launch traced here: 71.7 us
  Pallas kernels  71 us (99%)
    pallas_call x1, Pallas kernels, local(): pl.pallas_call(deliver, out_shape=tuple((jax.ShapeDtypeStruct(r.shape, r....  45.6 us
    pallas_call x1, Pallas kernels, local(): pl.pallas_call(functools.partial(kernel, n, ntp, heads, kv_dev, combiners...  25.5 us

profile of v3, /device:TPU:0, one launch (start us, length us, event | category | flops | bytes accessed | tf_op | source)
XLA Modules:
  0.0 71.7 jit_solution(14045853514361402805)
XLA Ops:
  0.6 25.5 %shard_map.120 = (bf16[128,3072]{1,0:T(8,128)(2,1)}, bf16[8,1536]{1,0:T(8,128)(2,1)}, bf16[1,256,640]{2,1,0:T(8,128)(2,1)}, bf16[1,256,640]{2,1,0:T(8,128)(2,1)}) custom-call(bf16[128,3072]{1,0:T(8,128)(2,1)} %q_hbm.1, bf16[128,1024]{1,0:T(8,128)(2,1)} %k_hbm.1, bf16[128,1024]{1,0:T(8,128)(2,1)} %v_hbm.1, s32[1,1024]{1,0:T(1,128)} %bitcast.1, s32[4]{0:T(128)} %rep_hbm.1, ...), custom_call_target="tpu_custom_call" | custom-call | tf_op jit(solution)/shard_map/pallas_call | solution.py:427
  26.1 45.6 %shard_map.121 = (bf16[128,3072]{1,0:T(8,128)(2,1)}, bf16[8,1536]{1,0:T(8,128)(2,1)}, bf16[1,256,640]{2,1,0:T(8,128)(2,1)}, bf16[1,256,640]{2,1,0:T(8,128)(2,1)}) custom-call(bf16[128,3072]{1,0:T(8,128)(2,1)} %get-tuple-element.8.refs_0_, bf16[8,1536]{1,0:T(8,128)(2,1)} %get-tuple-element.9.refs_1_, bf16[1,256,640]{2,1,0:T(8,128)(2,1)} %get-tuple-element.10.refs_2_, ...), custom_call_target="tpu_custom_call" | custom-call | tf_op jit(solution)/shard_map/pallas_call | solution.py:481

commit v4 on v3

--- a/solution.py
+++ b/solution.py
@@ -63,14 +63,50 @@
     ]
     for copy in small:
         copy.start()
-    q_copy.start()
-    w_copy.start()
 
     barrier = pltpu.get_barrier_semaphore()
     for t in range(1, n):
         pl.semaphore_signal(barrier, inc=1, device_id={"ctx": lax.rem(me + t, n)}, device_id_type=MESH)
     for t in range(1, ntp):
         pl.semaphore_signal(barrier, inc=1, device_id={"tp": lax.rem(tp + t, ntp)}, device_id_type=MESH)
+
+    pl.semaphore_wait(barrier, (n - 1) + (ntp - 1))
+
+    def move(way, owner, piece):
+        buf = (kbuf, vbuf)[piece]
+        target = (me + 2, me - 2, mate)[way]
+        return pltpu.make_async_remote_copy(
+            src_ref=buf.at[owner],
+            dst_ref=buf.at[owner],
+            send_sem=send_sem.at[way, owner, piece],
+            recv_sem=recv_sem.at[owner, piece],
+            device_id={"ctx": target},
+            device_id_type=MESH,
+        )
+
+    def move_own(way, piece):
+        target = (me + 2, me - 2, mate)[way]
+        return pltpu.make_async_remote_copy(
+            src_ref=(k_hbm, v_hbm)[piece].at[:, columns],
+            dst_ref=(kbuf, vbuf)[piece].at[me],
+            send_sem=send_sem.at[way, me, piece],
+            recv_sem=recv_sem.at[me, piece],
+            device_id={"ctx": target},
+            device_id_type=MESH,
+        )
+
+    for piece in range(2):
+        @pl.when(line < half - 1)
+        def _():
+            move_own(0, piece).start()
+
+        @pl.when(line > 0)
+        def _():
+            move_own(1, piece).start()
+
+        move_own(2, piece).start()
+    q_copy.start()
+    w_copy.start()
 
     for copy in small:
         copy.wait()
@@ -94,36 +130,9 @@
             sk_scr[g, low:low + ndoc, :] = sk_ref[:, head_columns].astype(F32)
             sv_scr[g, low:low + ndoc, :] = sv_ref[:, head_columns].astype(F32)
     att[...] = jnp.zeros(att.shape, F32)
-    tops[...] = jnp.full(tops.shape, -1e30, F32)
-    acc[...] = jnp.zeros(acc.shape, F32)
 
     k_copy.wait()
     v_copy.wait()
-    q_copy.wait()
-    pl.semaphore_wait(barrier, (n - 1) + (ntp - 1))
-
-    def move(way, owner, piece):
-        buf = (kbuf, vbuf)[piece]
-        target = (me + 2, me - 2, mate)[way]
-        return pltpu.make_async_remote_copy(
-            src_ref=buf.at[owner],
-            dst_ref=buf.at[owner],
-            send_sem=send_sem.at[way, owner, piece],
-            recv_sem=recv_sem.at[owner, piece],
-            device_id={"ctx": target},
-            device_id_type=MESH,
-        )
-
-    for piece in range(2):
-        @pl.when(line < half - 1)
-        def _():
-            move(0, me, piece).start()
-
-        @pl.when(line > 0)
-        def _():
-            move(1, me, piece).start()
-
-        move(2, me, piece).start()
 
     pairs = heads // 2
     group_pairs = pairs // kv_dev
@@ -178,6 +187,9 @@
         @pl.when(lax.rem(me + t, n) < combiners)
         def _():
             to_combiner(t).start()
+
+    tops[...] = jnp.full(tops.shape, -1e30, F32)
+    acc[...] = jnp.zeros(acc.shape, F32)
 
     def combine():
         comb[me] = part[pl.ds(me * share, share)]
@@ -257,7 +269,19 @@
                 + new.reshape(per, rows, 2 * HD)
             )
 
+    results = [
+        pltpu.make_async_copy(src, dst, out_sem.at[i])
+        for i, (src, dst) in enumerate((
+            (ctx_ref, ctx_hbm), (rk_ref, rk_hbm), (rv_ref, rv_hbm), (next_ref, next_hbm),
+        ))
+    ]
+    def finish():
+        for h in range(heads):
+            ctx_ref[:, h * HD:(h + 1) * HD] = (acc[h, :, 0:HD] / acc[h, :, HD:2 * HD]).astype(BF16)
+        results[0].start()
+
     back = 5 * n // 8
+    late = (line >= half - 1) & (2 * (line - half) + 3 >= me - back)
 
     def step(s, carry):
         low = line - s
@@ -288,6 +312,10 @@
         def _():
             project()
 
+        @pl.when((s == half) & jnp.logical_not(late))
+        def _():
+            finish()
+
         low = line - (s - 1)
         high = line + (s - 1)
 
@@ -305,24 +333,18 @@
         def _():
             group(low)
 
+        @pl.when((s == half) & late)
+        def _():
+            finish()
+
         @pl.when((s == 1) & (me < combiners))
         def _():
             combine()
 
         return carry
 
+    q_copy.wait()
     lax.fori_loop(1, half + 1, step, 0)
-
-    for h in range(heads):
-        ctx_ref[:, h * HD:(h + 1) * HD] = (acc[h, :, 0:HD] / acc[h, :, HD:2 * HD]).astype(BF16)
-
-    results = [
-        pltpu.make_async_copy(src, dst, out_sem.at[i])
-        for i, (src, dst) in enumerate((
-            (ctx_ref, ctx_hbm), (rk_ref, rk_hbm), (rv_ref, rv_hbm), (next_ref, next_hbm),
-        ))
-    ]
-    results[0].start()
 
     start = jnp.zeros((1, 1), F32)
     length = jnp.zeros((1, 1), F32)
@@ -401,10 +423,14 @@
 
 
 def deliver(*refs):
-    copies = [pltpu.make_async_copy(refs[i], refs[4 + i], refs[8].at[i]) for i in range(4)]
-    for copy in copies:
+    inward = [pltpu.make_async_copy(refs[i], refs[8 + i], refs[12].at[i]) for i in range(4)]
+    outward = [pltpu.make_async_copy(refs[8 + i], refs[4 + i], refs[12].at[4 + i]) for i in range(4)]
+    for copy in inward:
         copy.start()
-    for copy in copies:
+    for i in range(4):
+        inward[i].wait()
+        outward[i].start()
+    for copy in outward:
         copy.wait()
 
 
@@ -483,7 +509,7 @@
         out_shape=tuple(jax.ShapeDtypeStruct(r.shape, r.dtype) for r in results),
         in_specs=[hbm] * 4,
         out_specs=(hbm,) * 4,
-        scratch_shapes=[pltpu.SemaphoreType.DMA((4,))],
+        scratch_shapes=[pltpu.VMEM(r.shape, r.dtype) for r in results] + [pltpu.SemaphoreType.DMA((8,))],
         compiler_params=pltpu.CompilerParams(vmem_limit_bytes=60 * 1024 * 1024),
     )(*results)
 

time: 71.8 us -> 28.2 us (0.39)
  Pallas kernels: 71 us -> 27.4 us
    pallas_call x1, Pallas kernels: 45.6 us -> 2.3 us  [local(): pl.pallas_call(deliver, out_shape=tuple((jax.ShapeDtypeStruct(r.shape, r....]
where the time goes in v4:
time: 28.2 us; the launch traced here: 28.1 us
  Pallas kernels  27.4 us (97%)
  between operations  0.64 us (2%)
    pallas_call x1, Pallas kernels, local(): pl.pallas_call(functools.partial(kernel, n, ntp, heads, kv_dev, combiners...  25.1 us
    pallas_call x1, Pallas kernels, local(): pl.pallas_call(deliver, out_shape=tuple((jax.ShapeDtypeStruct(r.shape, r....  2.3 us

profile of v4, /device:TPU:0, one launch (start us, length us, event | category | flops | bytes accessed | tf_op | source)
XLA Modules:
  0.0 28.1 jit_solution(18299432895814013771)
XLA Ops:
  0.6 25.1 %shard_map.120 = (bf16[128,3072]{1,0:T(8,128)(2,1)}, bf16[8,1536]{1,0:T(8,128)(2,1)}, bf16[1,256,640]{2,1,0:T(8,128)(2,1)}, bf16[1,256,640]{2,1,0:T(8,128)(2,1)}) custom-call(bf16[128,3072]{1,0:T(8,128)(2,1)} %q_hbm.1, bf16[128,1024]{1,0:T(8,128)(2,1)} %k_hbm.1, bf16[128,1024]{1,0:T(8,128)(2,1)} %v_hbm.1, s32[1,1024]{1,0:T(1,128)} %bitcast.1, s32[4]{0:T(128)} %rep_hbm.1, ...), custom_call_target="tpu_custom_call" | custom-call | tf_op jit(solution)/shard_map/pallas_call | solution.py:453
  25.8 2.3 %shard_map.121 = (bf16[128,3072]{1,0:T(8,128)(2,1)}, bf16[8,1536]{1,0:T(8,128)(2,1)}, bf16[1,256,640]{2,1,0:T(8,128)(2,1)}, bf16[1,256,640]{2,1,0:T(8,128)(2,1)}) custom-call(bf16[128,3072]{1,0:T(8,128)(2,1)} %get-tuple-element.8.refs_0_, bf16[8,1536]{1,0:T(8,128)(2,1)} %get-tuple-element.9.refs_1_, bf16[1,256,640]{2,1,0:T(8,128)(2,1)} %get-tuple-element.10.refs_2_, ...), custom_call_target="tpu_custom_call" | custom-call | tf_op jit(solution)/shard_map/pallas_call | solution.py:507

commit v5 on v4

--- a/solution.py
+++ b/solution.py
@@ -30,7 +30,7 @@
     q_hbm, k_hbm, v_hbm, doc_hbm, rep_hbm, sq_hbm, sk_hbm, sv_hbm, w_hbm,
     ctx_hbm, next_hbm, rk_hbm, rv_hbm,
     kbuf, vbuf, qbuf, wbuf, acc, tops, bias, dstart, sq_scr, sk_scr, sv_scr, att, pack, cut, out_buf, in_buf,
-    part, comb, mixed, ctx_ref, next_ref, rk_ref, rv_ref, out_sem,
+    part, comb, mixed, pick, kt, vt, ctx_ref, next_ref, rk_ref, rv_ref, out_sem,
     doc_ref, rep_ref, sq_ref, sk_ref, sv_ref, local_sem, send_sem, recv_sem, part_send, part_recv, comb_send, comb_recv, mix_send, mix_recv,
 ):
     me = lax.axis_index("ctx")
@@ -191,6 +191,26 @@
     tops[...] = jnp.full(tops.shape, -1e30, F32)
     acc[...] = jnp.zeros(acc.shape, F32)
 
+    start = jnp.zeros((1, 1), F32)
+    length = jnp.zeros((1, 1), F32)
+    for d in range(ndoc):
+        named = rep_ref[d] == me
+        start = jnp.where(named, starts[d], start)
+        length = jnp.where(named, starts[d + 1] - starts[d], length)
+    slots = rk_ref.shape[2]
+    out_rows = rk_ref.shape[1]
+    chunk = slots // max(1, tokens // 1024)
+    for first in range(0, slots, chunk):
+        slot = (first + lax.broadcasted_iota(jnp.int32, (1, chunk), 1)).astype(F32)
+        source = jnp.where(slot < length, slot + start, -1.0)
+        position = lax.broadcasted_iota(jnp.int32, (tokens, chunk), 0).astype(F32)
+        pick[:, first:first + chunk] = jnp.where(position == source, 1.0, 0.0).astype(BF16)
+
+    def turn(o):
+        lanes = pl.ds(pl.multiple_of(2 * o * rows, 2 * rows), 2 * rows)
+        kt[:, lanes] = jnp.transpose(kbuf[pl.ds(2 * o, 2)].reshape(2 * rows, width))
+        vt[:, lanes] = jnp.transpose(vbuf[pl.ds(2 * o, 2)].reshape(2 * rows, width))
+
     def combine():
         comb[me] = part[pl.ds(me * share, share)]
         for t in range(1, n):
@@ -308,6 +328,10 @@
                     move(1, owner, piece).start()
 
                 move(2, owner, piece).start()
+        @pl.when((s == 1) & (me < combiners))
+        def _():
+            combine()
+
         @pl.when(s == half - 1)
         def _():
             project()
@@ -337,35 +361,25 @@
         def _():
             finish()
 
-        @pl.when((s == 1) & (me < combiners))
-        def _():
-            combine()
+        @pl.when(low >= 0)
+        def _():
+            turn(low)
+
+        @pl.when((high < half) & (s > 1))
+        def _():
+            turn(high)
 
         return carry
 
     q_copy.wait()
     lax.fori_loop(1, half + 1, step, 0)
 
-    start = jnp.zeros((1, 1), F32)
-    length = jnp.zeros((1, 1), F32)
-    for d in range(ndoc):
-        named = rep_ref[d] == me
-        start = jnp.where(named, starts[d], start)
-        length = jnp.where(named, starts[d + 1] - starts[d], length)
-    slots = rk_ref.shape[2]
-    out_rows = rk_ref.shape[1]
-    chunk = slots // max(1, tokens // 1024)
     for first in range(0, slots, chunk):
-        slot = (first + lax.broadcasted_iota(jnp.int32, (1, chunk), 1)).astype(F32)
-        source = jnp.where(slot < length, slot + start, -1.0)
-        position = lax.broadcasted_iota(jnp.int32, (tokens, chunk), 0).astype(F32)
-        pick = jnp.where(position == source, 1.0, 0.0).astype(BF16)
-        for buf, ref in ((kbuf, rk_ref), (vbuf, rv_ref)):
-            taken = dot(buf[...].reshape(tokens, width), pick, TN).astype(BF16)
+        for turned, ref in ((kt, rk_ref), (vt, rv_ref)):
+            taken = dot(turned[...], pick[:, first:first + chunk], NN).astype(BF16)
             if out_rows < width:
                 taken = jnp.where(tp % (width // out_rows) == 0, taken[0:out_rows], taken[out_rows:2 * out_rows])
             ref[0, :, first:first + chunk] = taken
-
     results[1].start()
     results[2].start()
 
@@ -480,6 +494,9 @@
             pltpu.VMEM((pairs, 8, 2 * HD), F32),
             pltpu.VMEM((n, pairs // combiners, 8, 2 * HD), F32),
             pltpu.VMEM((combiners, pairs // combiners, 8, HD), F32),
+            pltpu.VMEM((tokens, slots), BF16),
+            pltpu.VMEM((width, tokens), BF16),
+            pltpu.VMEM((width, tokens), BF16),
             pltpu.VMEM((rows, depth), BF16),
             pltpu.VMEM((n, out_columns), BF16),
             pltpu.VMEM((1, share, slots), BF16),

time: 28.2 us -> 29 us (1.028)
  Pallas kernels: 27.4 us -> 28.3 us
    pallas_call x1, Pallas kernels: 25.1 us -> 26 us  [local(): pl.pallas_call(functools.partial(kernel, n, ntp, heads, kv_dev, combiners...]
where the time goes in v5:
time: 29 us; the launch traced here: 28.9 us
  Pallas kernels  28.3 us (98%)
  between operations  0.64 us (2%)
    pallas_call x1, Pallas kernels, local(): pl.pallas_call(functools.partial(kernel, n, ntp, heads, kv_dev, combiners...  26 us
    pallas_call x1, Pallas kernels, local(): pl.pallas_call(deliver, out_shape=tuple((jax.ShapeDtypeStruct(r.shape, r....  2.3 us

profile of v5, /device:TPU:0, one launch (start us, length us, event | category | flops | bytes accessed | tf_op | source)
XLA Modules:
  0.0 28.9 jit_solution(8058189794585099550)
XLA Ops:
  0.6 26.0 %shard_map.120 = (bf16[128,3072]{1,0:T(8,128)(2,1)}, bf16[8,1536]{1,0:T(8,128)(2,1)}, bf16[1,256,640]{2,1,0:T(8,128)(2,1)}, bf16[1,256,640]{2,1,0:T(8,128)(2,1)}) custom-call(bf16[128,3072]{1,0:T(8,128)(2,1)} %q_hbm.1, bf16[128,1024]{1,0:T(8,128)(2,1)} %k_hbm.1, bf16[128,1024]{1,0:T(8,128)(2,1)} %v_hbm.1, s32[1,1024]{1,0:T(1,128)} %bitcast.1, s32[4]{0:T(128)} %rep_hbm.1, ...), custom_call_target="tpu_custom_call" | custom-call | tf_op jit(solution)/shard_map/pallas_call | solution.py:467
  26.6 2.3 %shard_map.121 = (bf16[128,3072]{1,0:T(8,128)(2,1)}, bf16[8,1536]{1,0:T(8,128)(2,1)}, bf16[1,256,640]{2,1,0:T(8,128)(2,1)}, bf16[1,256,640]{2,1,0:T(8,128)(2,1)}) custom-call(bf16[128,3072]{1,0:T(8,128)(2,1)} %get-tuple-element.8.refs_0_, bf16[8,1536]{1,0:T(8,128)(2,1)} %get-tuple-element.9.refs_1_, bf16[1,256,640]{2,1,0:T(8,128)(2,1)} %get-tuple-element.10.refs_2_, ...), custom_call_target="tpu_custom_call" | custom-call | tf_op jit(solution)/shard_map/pallas_call | solution.py:524

commit v6 on v4

--- a/solution.py
+++ b/solution.py
@@ -26,12 +26,12 @@
 
 
 def kernel(
-    n, ntp, heads, kv_dev, combiners,
+    n, ntp, heads, kv_dev,
     q_hbm, k_hbm, v_hbm, doc_hbm, rep_hbm, sq_hbm, sk_hbm, sv_hbm, w_hbm,
     ctx_hbm, next_hbm, rk_hbm, rv_hbm,
     kbuf, vbuf, qbuf, wbuf, acc, tops, bias, dstart, sq_scr, sk_scr, sv_scr, att, pack, cut, out_buf, in_buf,
-    part, comb, mixed, ctx_ref, next_ref, rk_ref, rv_ref, out_sem,
-    doc_ref, rep_ref, sq_ref, sk_ref, sv_ref, local_sem, send_sem, recv_sem, part_send, part_recv, comb_send, comb_recv, mix_send, mix_recv,
+    mixed, ctx_ref, next_ref, rk_ref, rv_ref, out_sem,
+    doc_ref, rep_ref, sq_ref, sk_ref, sv_ref, local_sem, send_sem, recv_sem, part_send, part_recv,
 ):
     me = lax.axis_index("ctx")
     tp = lax.axis_index("tp")
@@ -136,92 +136,33 @@
 
     pairs = heads // 2
     group_pairs = pairs // kv_dev
-    share = pairs // combiners
-    shape = (group_pairs * 8, rows)
-    row_doc = (lax.broadcasted_iota(jnp.int32, shape, 0) % ndoc).astype(F32)
-    inside = row_doc == own_docs
-    for g in range(kv_dev):
-        lanes = slice(g * HD, (g + 1) * HD)
-        q = sq_scr[g * group_pairs:(g + 1) * group_pairs].reshape(group_pairs * 8, HD).astype(BF16)
-        s = dot(q, kbuf[me, :, lanes], NT)
-        top = jnp.max(jnp.where(inside, s, -1e30), axis=1, keepdims=True)
-        weights = jnp.where(inside, jnp.exp2((s - top) * EXP_SCALE), 0.0)
-        total = jnp.sum(weights, axis=1, keepdims=True)
-        summed = dot(weights.astype(BF16), vbuf[me, :, lanes], NN)
-        half_lane = lax.broadcasted_iota(jnp.int32, (group_pairs * 8, HD), 1) < HD // 2
-        both = jnp.concatenate([summed, jnp.where(half_lane, top, total)], axis=1)
-        part[g * group_pairs:(g + 1) * group_pairs] = both.reshape(group_pairs, 8, 2 * HD)
-
-    def to_combiner(t):
-        target = lax.rem(me + t, n)
-        return pltpu.make_async_remote_copy(
-            src_ref=part.at[pl.ds(jnp.minimum(target, combiners - 1) * share, share)],
-            dst_ref=comb.at[me],
-            send_sem=comb_send.at[t],
-            recv_sem=comb_recv.at[me],
-            device_id={"ctx": target},
-            device_id_type=MESH,
-        )
-
-    def from_device(sender):
-        return pltpu.make_async_remote_copy(
-            src_ref=comb.at[sender],
-            dst_ref=comb.at[sender],
-            send_sem=comb_send.at[0],
-            recv_sem=comb_recv.at[sender],
-            device_id={"ctx": mate},
-            device_id_type=MESH,
-        )
-
-    def mix_copy(t, slot):
-        return pltpu.make_async_remote_copy(
-            src_ref=mixed.at[slot],
-            dst_ref=mixed.at[slot],
-            send_sem=mix_send.at[t],
-            recv_sem=mix_recv.at[slot],
-            device_id={"ctx": lax.rem(me + t, n)},
-            device_id_type=MESH,
-        )
-
-    for t in range(1, n):
-        @pl.when(lax.rem(me + t, n) < combiners)
-        def _():
-            to_combiner(t).start()
-
     tops[...] = jnp.full(tops.shape, -1e30, F32)
     acc[...] = jnp.zeros(acc.shape, F32)
 
-    def combine():
-        comb[me] = part[pl.ds(me * share, share)]
-        for t in range(1, n):
-            from_device(lax.rem(me + t, n)).wait_recv()
-        for j in range(share):
-            pair = me * share + j
-            g = pair // group_pairs
-            own = jnp.sum(sq_scr[pair] * sk_scr[g], axis=1, keepdims=True)
-            top = own
-            for i in range(n):
-                top = jnp.maximum(top, comb[i, j, :, HD:HD + 1])
+    def decode():
+        shape = (group_pairs * 8, tokens)
+        row_doc = (lax.broadcasted_iota(jnp.int32, shape, 0) % ndoc).astype(F32)
+        inside = row_doc == docs
+        for g in range(kv_dev):
+            lanes = slice(g * HD, (g + 1) * HD)
+            q = sq_scr[g * group_pairs:(g + 1) * group_pairs]
+            own = jnp.sum(q * sk_scr[g][None], axis=2, keepdims=True).reshape(group_pairs * 8, 1)
+            q = q.reshape(group_pairs * 8, HD).astype(BF16)
+            s = dot(q, kbuf[:, :, lanes].reshape(tokens, HD), NT)
+            top = jnp.maximum(jnp.max(jnp.where(inside, s, -1e30), axis=1, keepdims=True), own)
+            weights = jnp.where(inside, jnp.exp2((s - top) * EXP_SCALE), 0.0)
             own_weight = jnp.exp2((own - top) * EXP_SCALE)
-            total = own_weight
-            summed = own_weight.astype(BF16).astype(F32) * sv_scr[g]
-            for i in range(n):
-                fade = jnp.exp2((comb[i, j, :, HD:HD + 1] - top) * EXP_SCALE)
-                total = total + fade * comb[i, j, :, HD + HD // 2:HD + HD // 2 + 1]
-                summed = summed + fade * comb[i, j, :, 0:HD]
-            mixed[me, j] = summed / total
-        for t in range(1, n):
-            mix_copy(t, me).start()
+            total = jnp.sum(weights, axis=1, keepdims=True) + own_weight
+            own_value = jnp.broadcast_to(sv_scr[g][None], (group_pairs, 8, HD)).reshape(group_pairs * 8, HD)
+            summed = dot(weights.astype(BF16), vbuf[:, :, lanes].reshape(tokens, HD), NN)
+            summed = (summed + own_weight.astype(BF16).astype(F32) * own_value) / total
+            mixed[g * group_pairs:(g + 1) * group_pairs] = summed.reshape(group_pairs, 8, HD)
 
     def project():
-        for c in range(combiners):
-            @pl.when(c != me)
-            def _():
-                mix_copy(1, c).wait_recv()
         for h in range(heads):
             low = h % 2 * ndoc
             pair = h // 2
-            att[0:ndoc, h * HD:(h + 1) * HD] = mixed[pair // share, pair % share, low:low + ndoc, :]
+            att[0:ndoc, h * HD:(h + 1) * HD] = mixed[pair, low:low + ndoc, :]
         w_copy.wait()
         rows_in = att[...].astype(BF16)
         for c in range(pieces):
@@ -308,10 +249,6 @@
                     move(1, owner, piece).start()
 
                 move(2, owner, piece).start()
-        @pl.when(s == half - 1)
-        def _():
-            project()
-
         @pl.when((s == half) & jnp.logical_not(late))
         def _():
             finish()
@@ -337,14 +274,12 @@
         def _():
             finish()
 
-        @pl.when((s == 1) & (me < combiners))
-        def _():
-            combine()
-
         return carry
 
     q_copy.wait()
     lax.fori_loop(1, half + 1, step, 0)
+    decode()
+    project()
 
     start = jnp.zeros((1, 1), F32)
     length = jnp.zeros((1, 1), F32)
@@ -383,15 +318,6 @@
     results[3].start()
     for t in range(1, ntp):
         term(t).wait_send()
-    for t in range(1, n):
-        @pl.when(lax.rem(me + t, n) < combiners)
-        def _():
-            to_combiner(t).wait_send()
-
-        @pl.when(me < combiners)
-        def _():
-            mix_copy(t, me).wait_send()
-
     def drain(s, carry):
         for piece in range(2):
             @pl.when(line - s >= 0)
@@ -449,9 +375,8 @@
     hbm = pl.BlockSpec(memory_space=pl.ANY)
     share = keys.shape[1] // ntp
     pairs = heads // 2
-    combiners = max(c for c in range(1, n + 1) if pairs % c == 0)
     results = pl.pallas_call(
-        functools.partial(kernel, n, ntp, heads, kv_dev, combiners),
+        functools.partial(kernel, n, ntp, heads, kv_dev),
         out_shape=(
             jax.ShapeDtypeStruct((rows, depth), BF16),
             jax.ShapeDtypeStruct((n, out_columns), BF16),
@@ -477,9 +402,7 @@
             pltpu.VMEM((pieces, 8, size), F32),
             pltpu.VMEM((16, size), BF16),
             pltpu.VMEM((ntp, 16, size), BF16),
-            pltpu.VMEM((pairs, 8, 2 * HD), F32),
-            pltpu.VMEM((n, pairs // combiners, 8, 2 * HD), F32),
-            pltpu.VMEM((combiners, pairs // combiners, 8, HD), F32),
+            pltpu.VMEM((pairs, 8, HD), F32),
             pltpu.VMEM((rows, depth), BF16),
             pltpu.VMEM((n, out_columns), BF16),
             pltpu.VMEM((1, share, slots), BF16),
@@ -495,10 +418,6 @@
             pltpu.SemaphoreType.DMA((n, 2)),
             pltpu.SemaphoreType.DMA((ntp,)),
             pltpu.SemaphoreType.DMA((ntp,)),
-            pltpu.SemaphoreType.DMA((n,)),
-            pltpu.SemaphoreType.DMA((n,)),
-            pltpu.SemaphoreType.DMA((n,)),
-            pltpu.SemaphoreType.DMA((n,)),
         ],
         compiler_params=pltpu.CompilerParams(
             collective_id=0, has_side_effects=True, vmem_limit_bytes=60 * 1024 * 1024

time: 28.2 us -> 29.6 us (1.050)
  Pallas kernels: 27.4 us -> 28.8 us
    pallas_call x1, Pallas kernels: 25.1 us -> 26.5 us  [local(): pl.pallas_call(functools.partial(kernel, n, ntp, heads, kv_dev), out_shap...]
where the time goes in v6:
time: 29.6 us; the launch traced here: 29.4 us
  Pallas kernels  28.8 us (97%)
  between operations  0.64 us (2%)
    pallas_call x1, Pallas kernels, local(): pl.pallas_call(functools.partial(kernel, n, ntp, heads, kv_dev), out_shap...  26.5 us
    pallas_call x1, Pallas kernels, local(): pl.pallas_call(deliver, out_shape=tuple((jax.ShapeDtypeStruct(r.shape, r....  2.3 us

profile of v6, /device:TPU:0, one launch (start us, length us, event | category | flops | bytes accessed | tf_op | source)
XLA Modules:
  0.0 29.4 jit_solution(7636455863849898790)
XLA Ops:
  0.6 26.5 %shard_map.120 = (bf16[128,3072]{1,0:T(8,128)(2,1)}, bf16[8,1536]{1,0:T(8,128)(2,1)}, bf16[1,256,640]{2,1,0:T(8,128)(2,1)}, bf16[1,256,640]{2,1,0:T(8,128)(2,1)}) custom-call(bf16[128,3072]{1,0:T(8,128)(2,1)} %q_hbm.1, bf16[128,1024]{1,0:T(8,128)(2,1)} %k_hbm.1, bf16[128,1024]{1,0:T(8,128)(2,1)} %v_hbm.1, s32[1,1024]{1,0:T(1,128)} %bitcast.1, s32[4]{0:T(128)} %rep_hbm.1, ...), custom_call_target="tpu_custom_call" | custom-call | tf_op jit(solution)/shard_map/pallas_call | solution.py:378
  27.1 2.3 %shard_map.121 = (bf16[128,3072]{1,0:T(8,128)(2,1)}, bf16[8,1536]{1,0:T(8,128)(2,1)}, bf16[1,256,640]{2,1,0:T(8,128)(2,1)}, bf16[1,256,640]{2,1,0:T(8,128)(2,1)}) custom-call(bf16[128,3072]{1,0:T(8,128)(2,1)} %get-tuple-element.8.refs_0_, bf16[8,1536]{1,0:T(8,128)(2,1)} %get-tuple-element.9.refs_1_, bf16[1,256,640]{2,1,0:T(8,128)(2,1)} %get-tuple-element.10.refs_2_, ...), custom_call_target="tpu_custom_call" | custom-call | tf_op jit(solution)/shard_map/pallas_call | solution.py:426
